TPU v7x, 128 devices: a whole 4x4x4 slice. The times are simulated.
128 devices in a mesh: row: 8 (over z, y_lo), chan: 16 (over x, y_hi, core).
Axes of the slice: x: 4, y: 4 (y_hi: 2, y_lo: 2; y = y_hi * 2 + y_lo), z: 4, core: 2. Of those that a mesh axis runs over, the one named last changes fastest.
Arguments:
- pair: bfloat16 [128, 512, 512], P('chan', 'row'), may hold values from -6 to 6
- grad_out: bfloat16 [128, 512, 512], P('chan', 'row'), may hold values from -6 to 6
- residue_chain: int32 [512], replicated, may hold values from 0 to 4, as said below
- gain_in: float32 [2, 128], replicated, may hold values from 0.25 to 1.75
- w_in: bfloat16 [2, 128, 640], replicated, may hold values from -0.5 to 0.5
- gain_mid: float32 [2, 128], replicated, may hold values from 0.25 to 1.75
- w_out: bfloat16 [2, 128, 128], replicated, may hold values from -0.5 to 0.5
Outputs:
- pair_out: bfloat16 [128, 512, 512], P('chan', 'row')
- grad_pair: bfloat16 [128, 512, 512], P('chan', 'row')
- grad_gain_in: float32 [2, 128], replicated
- grad_w_in: float32 [2, 128, 640], replicated
- grad_gain_mid: float32 [2, 128], replicated
- grad_w_out: float32 [2, 128, 128], replicated
Inputs may be any that keep to these rules, and one draw needn't show every extreme that they name: `residue_chain`: padding (0) fills a run of 1 to 64 residues at the end of the crop; every other residue is valid.
All inputs are finite; a program needn't handle non-finite values.
Results may differ from a plain program's by a relative error of at most 0.023.
Values may be sent and summed in bfloat16 or wider, within the bound.
A program may use at most 128 MiB of HBM per device.

v0:
```python
from functools import partial

import jax
import jax.numpy as jnp
from jax import lax
from jax.sharding import PartitionSpec as P

epsilon = 1e-05
highest = lax.Precision.HIGHEST


def normalize(values, gain_vec):
    center = values - jnp.mean(values, axis=0, keepdims=True)
    spread = jnp.mean(center * center, axis=0, keepdims=True)
    return center * lax.rsqrt(spread + epsilon) * gain_vec[:, None, None]


def prepare(pair_f32, gain_vec, weight, mask_f):
    hidden_w = (weight.shape[1] - pair_f32.shape[0]) // 4
    normed = normalize(pair_f32, gain_vec)
    project = jnp.einsum("cd,cij->dij", weight, normed, precision=highest)
    left_proj = (
        mask_f * jax.nn.sigmoid(project[hidden_w : 2 * hidden_w]) * project[:hidden_w]
    ).astype(jnp.bfloat16)
    right_proj = (
        mask_f
        * jax.nn.sigmoid(project[3 * hidden_w : 4 * hidden_w])
        * project[2 * hidden_w : 3 * hidden_w]
    ).astype(jnp.bfloat16)
    gate_bf = jax.nn.sigmoid(project[4 * hidden_w :]).astype(jnp.bfloat16)
    return (left_proj, right_proj, gate_bf)


def finish(pair_f32, mixture, gate_bf, gain_vec, weight):
    normed = normalize(mixture.astype(jnp.float32), gain_vec)
    update = jnp.einsum("hc,hij->cij", weight, normed, precision=highest)
    return (pair_f32 + gate_bf.astype(jnp.float32) * update).astype(jnp.bfloat16)


def to_columns(left_proj, right_proj):
    return (
        lax.all_to_all(left_proj, "chan", split_axis=0, concat_axis=1, tiled=True),
        lax.all_to_all(right_proj, "chan", split_axis=0, concat_axis=1, tiled=True),
    )


def to_rows(mixture):
    return lax.all_to_all(mixture, "chan", split_axis=1, concat_axis=0, tiled=True)


def from_rows(cotangent):
    return lax.all_to_all(cotangent, "chan", split_axis=0, concat_axis=1, tiled=True)


def back_to_rows(grad_left, grad_right):
    return (
        lax.all_to_all(grad_left, "chan", split_axis=1, concat_axis=0, tiled=True),
        lax.all_to_all(grad_right, "chan", split_axis=1, concat_axis=0, tiled=True),
    )


def local(pair, grad_out, residue_chain, gain_in, w_in, gain_mid, w_out):
    groups = lax.axis_size("chan")
    own_rows = pair.shape[1]
    slab_rows = own_rows // groups
    first_row = lax.axis_index("row") * own_rows + lax.axis_index("chan") * slab_rows
    validity = (residue_chain > 0).astype(jnp.float32)
    mask_f = lax.dynamic_slice_in_dim(validity, first_row, slab_rows)[:, None] * validity[None, :]
    weights_in = w_in.astype(jnp.float32)
    weights_out = w_out.astype(jnp.float32)
    prepare_masked = partial(prepare, mask_f=mask_f)
    field_now, cotangent = (
        lax.all_to_all(pair, "chan", split_axis=1, concat_axis=0, tiled=True),
        lax.all_to_all(grad_out, "chan", split_axis=1, concat_axis=0, tiled=True),
    )
    pair_zero = field_now.astype(jnp.float32)
    left_zero, right_zero, gate_zero = prepare_masked(pair_zero, gain_in[0], weights_in[0])
    left_a, right_a = to_columns(left_zero, right_zero)
    mixture_zero = jnp.einsum(
        "hik,hjk->hij",
        left_a,
        lax.all_gather(right_a, "row", axis=1, tiled=True),
        preferred_element_type=jnp.float32,
    ).astype(jnp.bfloat16)
    mix_rows_zero = to_rows(mixture_zero)
    field_one = finish(pair_zero, mix_rows_zero, gate_zero, gain_mid[0], weights_out[0])
    pair_one = field_one.astype(jnp.float32)
    left_one, right_one, gate_one = prepare_masked(pair_one, gain_in[1], weights_in[1])
    left_b, right_b = to_columns(left_one, right_one)
    columns = left_b
    mixture_one = jnp.transpose(
        lax.psum_scatter(
            jnp.einsum("hki,hkj->ihj", columns, right_b, preferred_element_type=jnp.float32).astype(
                jnp.bfloat16
            ),
            "row",
            scatter_dimension=0,
            tiled=True,
        ).astype(jnp.float32),
        (1, 0, 2),
    )
    mix_rows_one = to_rows(mixture_one.astype(jnp.bfloat16))
    field_two = finish(pair_one, mix_rows_one, gate_one, gain_mid[1], weights_out[1])
    _, pull_finish_one = jax.vjp(
        finish, pair_one, mix_rows_one, gate_one, gain_mid[1], weights_out[1]
    )
    dfield_fin1, dmix_one, dgate_one, dgm_one, dwo_one = pull_finish_one(cotangent)
    dmix_one_a = from_rows(dmix_one)
    portion = lax.all_gather(dmix_one_a, "row", axis=1, tiled=True)
    columns = left_b
    grad_right = jnp.einsum("hki,hij->hkj", columns, portion, preferred_element_type=jnp.float32)
    product = jnp.einsum("hkj,hij->hki", right_b, portion, preferred_element_type=jnp.float32)
    dleft_one, dright_one = back_to_rows(
        product.astype(jnp.bfloat16), grad_right.astype(jnp.bfloat16)
    )
    _, pull_prepare_one = jax.vjp(prepare_masked, pair_one, gain_in[1], weights_in[1])
    dfield_pre1, dgi_one, dwi_one = pull_prepare_one((dleft_one, dright_one, dgate_one))
    grad_field_one = (dfield_fin1 + dfield_pre1).astype(jnp.bfloat16)
    _, pull_finish_zero = jax.vjp(
        finish, pair_zero, mix_rows_zero, gate_zero, gain_mid[0], weights_out[0]
    )
    dfield_fin0, dmix_zero, dgate_zero, dgm_zero, dwo_zero = pull_finish_zero(grad_field_one)
    dmix_zero_a = from_rows(dmix_zero)
    columns = dmix_zero_a
    grad_left_zero = jnp.einsum(
        "hij,hjk->hik",
        columns,
        lax.all_gather(right_a, "row", axis=1, tiled=True),
        preferred_element_type=jnp.float32,
    )
    columns = dmix_zero_a
    grad_right_zero = jnp.transpose(
        lax.psum_scatter(
            jnp.einsum("hij,hik->jhk", columns, left_a, preferred_element_type=jnp.float32).astype(
                jnp.bfloat16
            ),
            "row",
            scatter_dimension=0,
            tiled=True,
        ).astype(jnp.float32),
        (1, 0, 2),
    )
    dleft_zero, dright_zero = back_to_rows(
        grad_left_zero.astype(jnp.bfloat16), grad_right_zero.astype(jnp.bfloat16)
    )
    _, pull_prepare_zero = jax.vjp(prepare_masked, pair_zero, gain_in[0], weights_in[0])
    dfield_pre0, dgi_zero, dwi_zero = pull_prepare_zero((dleft_zero, dright_zero, dgate_zero))
    grad_field_zero = (dfield_fin0 + dfield_pre0).astype(jnp.bfloat16)
    pair_out, grad_pair = (
        lax.all_to_all(field_two, "chan", split_axis=0, concat_axis=1, tiled=True),
        lax.all_to_all(grad_field_zero, "chan", split_axis=0, concat_axis=1, tiled=True),
    )
    summed = lax.psum(
        (
            jnp.stack([dgi_zero, dgi_one]),
            jnp.stack([dwi_zero, dwi_one]),
            jnp.stack([dgm_zero, dgm_one]),
            jnp.stack([dwo_zero, dwo_one]),
        ),
        ("row", "chan"),
    )
    factor = 1.0 / pair.shape[2]
    return (
        pair_out,
        grad_pair,
        summed[0] * factor,
        summed[1] * factor,
        summed[2] * factor,
        summed[3] * factor,
    )


def solution(mesh):
    return jax.shard_map(
        local,
        mesh=mesh,
        in_specs=(P("chan", "row", None), P("chan", "row", None), P(), P(), P(), P(), P()),
        out_specs=(P("chan", "row", None), P("chan", "row", None), P(), P(), P(), P()),
        check_vma=False,
    )
```

profile of v0, /device:TPU:1, one launch (start us, length us, event | category | flops | bytes accessed | tf_op | source)
XLA Modules:
  0.0 834.7 jit_solution(17164236661705597763)
XLA Ops:
  9.3 8.4 %all-to-all-start = ((bf16[8,64,512]{2,0,1:T(8,128)(2,1)}), bf16[8,64,512]{2,0,1:T(8,128)(2,1)S(1)}, u32[]{:S(2)}, u32[]{:S(2)}) async-start(bf16[8,64,512]{2,0,1:T(8,128)(2,1)} %copy.234), calls=%async_computation | async-start | bytes 1048576 | tf_op jit(solution)/shard_map/all_to_all | solution.py:73
  20.0 8.9 %all-to-all-done = bf16[8,64,512]{2,0,1:T(8,128)(2,1)S(1)} async-done(((bf16[8,64,512]{2,0,1:T(8,128)(2,1)}), bf16[8,64,512]{2,0,1:T(8,128)(2,1)S(1)}, u32[]{:S(2)}, u32[]{:S(2)}) %all-to-all-start) | async-done | bytes 524320 | tf_op jit(solution)/shard_map/all_to_all | solution.py:73
  35.8 15.0 %all_to_all.216 = bf16[128,4,512]{2,1,0:T(4,128)(2,1)S(1)} all-to-all(bf16[128,4,512]{2,1,0:T(4,128)(2,1)S(1)} %copy.241), channel_id=1, replica_groups=mesh['row'=8,'chan'=16] {'chan'}, dimensions={0} | all-to-all | bytes 1048576 | tf_op jit(solution)/shard_map/all_to_all | solution.py:43
  52.6 15.0 %all_to_all.217 = bf16[128,4,512]{2,1,0:T(4,128)(2,1)S(1)} all-to-all(bf16[128,4,512]{2,1,0:T(4,128)(2,1)S(1)} %copy.238), channel_id=1, replica_groups=mesh['row'=8,'chan'=16] {'chan'}, dimensions={0} | all-to-all | bytes 1048576 | tf_op jit(solution)/shard_map/all_to_all | solution.py:42
  68.2 77.6 %all-gather.3.cloned.1.call-done = bf16[8,512,512]{2,1,0:T(8,128)(2,1)} async-done(((bf16[8,64,512]{2,1,0:T(8,128)(2,1)}), bf16[8,512,512]{2,1,0:T(8,128)(2,1)}) %all-gather.3.cloned.1.call-update) | async-done | bytes 4194320 | tf_op jit(solution)/shard_map/all_gather | solution.py:82
  150.5 7.8 all-to-all-start.3
  162.1 7.2 all-to-all-done.3
  182.3 5.3 all-to-all-start.4
  188.8 10.1 %all-to-all-done.4 = bf16[128,4,512]{2,1,0:T(4,128)(2,1)} async-done(((bf16[128,4,512]{2,1,0:T(4,128)(2,1)}), bf16[128,4,512]{2,1,0:T(4,128)(2,1)}, u32[]{:S(2)}, u32[]{:S(2)}) %all-to-all-start.4) | async-done | bytes 524320 | tf_op jit(solution)/shard_map/all_to_all | solution.py:43
  198.9 5.3 all-to-all-start.5
  207.8 7.7 all-to-all-done.5
  224.2 8.0 copy.255
  233.6 15.6 %all_to_all.218 = bf16[8,64,512]{2,0,1:T(8,128)(2,1)} all-to-all(bf16[8,64,512]{2,0,1:T(8,128)(2,1)S(1)} %copy.261), channel_id=1, replica_groups=mesh['row'=8,'chan'=16] {'chan'}, dimensions={1} | all-to-all | bytes 1048576 | tf_op jit(solution)/shard_map/all_to_all | solution.py:74
  249.2 75.3 %reduce-scatter.3.cloned.1.call-done = bf16[64,8,512]{2,1,0:T(8,128)(2,1)} async-done(((bf16[512,8,512]{2,1,0:T(8,128)(2,1)}), bf16[64,8,512]{2,1,0:T(8,128)(2,1)}) %reduce-scatter.3.cloned.1.call-update) | async-done | bytes 524304 | tf_op jit(solution)/shard_map/reduce_scatter | solution.py:92
  324.5 7.2 all-to-all-start.6
  336.8 6.1 all-to-all-done.6
  348.4 15.0 %all_to_all.219 = bf16[128,4,512]{2,1,0:T(4,128)(2,1)S(1)} all-to-all(bf16[128,4,512]{2,1,0:T(4,128)(2,1)S(1)} %copy.267), channel_id=1, replica_groups=mesh['row'=8,'chan'=16] {'chan'}, dimensions={0} | all-to-all | bytes 1048576 | tf_op jit(solution)/shard_map/all_to_all | solution.py:52
  366.4 88.8 %all-gather.5.cloned.1.call-done = bf16[8,512,512]{2,1,0:T(8,128)(2,1)} async-done(((bf16[8,64,512]{2,1,0:T(8,128)(2,1)}), bf16[8,512,512]{2,1,0:T(8,128)(2,1)}) %all-gather.5.cloned.1.call-update) | async-done | bytes 4194320 | tf_op jit(solution)/shard_map/all_gather | solution.py:109
  459.5 7.4 all-to-all-start.10
  471.6 6.4 all-to-all-done.10
  478.1 5.3 all-to-all-start.11
  489.4 5.3 all-to-all-done.11
  499.3 5.4 fusion.22
  517.2 15.0 %all_to_all.220 = bf16[128,4,512]{2,1,0:T(4,128)(2,1)S(1)} all-to-all(bf16[128,4,512]{2,1,0:T(4,128)(2,1)S(1)} %copy.282), channel_id=1, replica_groups=mesh['row'=8,'chan'=16] {'chan'}, dimensions={0} | all-to-all | bytes 1048576 | tf_op jit(solution)/shard_map/all_to_all | solution.py:52
  536.9 8.1 copy.284
  546.2 5.9 all-to-all-start.7
  557.8 5.5 all-to-all-done.7
  580.0 63.8 %reduce-scatter.5.cloned.1.call-done = bf16[64,8,512]{2,1,0:T(8,128)(2,1)} async-done(((bf16[512,8,512]{2,1,0:T(8,128)(2,1)}), bf16[64,8,512]{2,1,0:T(8,128)(2,1)}) %reduce-scatter.5.cloned.1.call-update) | async-done | bytes 524304 | tf_op jit(solution)/shard_map/reduce_scatter | solution.py:133
  643.8 7.7 all-to-all-start.13
  657.2 5.4 all-to-all-done.13
  685.8 65.7 %all-reduce.10 = (f32[2,128]{1,0:T(2,128)S(1)}, f32[2,128]{1,0:T(2,128)S(1)}) all-reduce(f32[2,128]{1,0:T(2,128)S(1)} %pad_maximum_fusion.2, f32[2,128]{1,0:T(2,128)S(1)} %pad_maximum_fusion.3), channel_id=1, replica_groups=mesh['row'=8,'chan'=16] {'row','chan'}, use_global_device_ids=true, to_apply=%region_20.0 | all-reduce | flops 512 | bytes 4096 | tf_op jit(solution)/shard_map/psum | solution.py:153
  752.0 71.4 %all-reduce.14.cloned.1.call-done = (f32[2,128,640]{2,1,0:T(8,128)}, f32[2,128,128]{2,1,0:T(8,128)}) async-done(((f32[2,128,640]{2,1,0:T(8,128)}, f32[2,128,128]{2,1,0:T(8,128)}), (f32[2,128,640]{2,1,0:T(8,128)}, f32[2,128,128]{2,1,0:T(8,128)})) %all-reduce.14.cloned.1.call-update) | async-done | bytes 786448 | tf_op jit(solution)/shard_map/psum | solution.py:153
  (217 shorter events, 157.4 us)
Async XLA Ops:
  9.3 19.6 %all-to-all-start = ((bf16[8,64,512]{2,0,1:T(8,128)(2,1)}), bf16[8,64,512]{2,0,1:T(8,128)(2,1)S(1)}, u32[]{:S(2)}, u32[]{:S(2)}) async-start(bf16[8,64,512]{2,0,1:T(8,128)(2,1)} %copy.234), calls=%async_computation | async-start | bytes 1048576 | tf_op jit(solution)/shard_map/all_to_all | solution.py:73
  17.7 128.1 %all-gather.3.cloned.1.call-start = ((), (), s32[]{:S(2)}) async-start(), calls=%async_computation.18 | async-start | bytes 4718592 | tf_op jit(solution)/shard_map/all_gather | solution.py:82
  19.1 154.8 %copy-start.22 = (f32[128]{0:T(128)}, f32[128]{0:T(128)S(1)}, u32[]{:S(2)}) copy-start(f32[128]{0:T(128)S(1)} %get-tuple-element.67) | copy-start | bytes 1540
  67.6 90.7 %copy-start.32 = (f32[2,128]{1,0:T(2,128)S(1)}, f32[2,128]{1,0:T(2,128)}, u32[]{:S(2)}) copy-start(f32[2,128]{1,0:T(2,128)} %param.12) | copy-start | bytes 3076
  68.2 93.9 %copy-start.6 = (bf16[8,64,512]{2,1,0:T(8,128)(2,1)}, bf16[8,64,512]{2,1,0:T(8,128)(2,1)S(1)}, u32[]{:S(2)}) copy-start(bf16[8,64,512]{2,1,0:T(8,128)(2,1)S(1)} %all_to_all.164) | copy-start | bytes 1572868
  150.5 18.9 %all-to-all-start.3 = ((bf16[8,64,512]{2,0,1:T(8,128)(2,1)}), bf16[8,64,512]{2,0,1:T(8,128)(2,1)S(1)}, u32[]{:S(2)}, u32[]{:S(2)}) async-start(bf16[8,64,512]{2,0,1:T(8,128)(2,1)} %copy.244), calls=%async_computation.3 | async-start | bytes 1048576 | tf_op jit(solution)/shard_map/all_to_all | solution.py:48
  162.1 11.8 %copy-start.14 = (bf16[2,128,640]{2,1,0:T(8,128)(2,1)S(1)}, bf16[2,128,640]{2,1,0:T(8,128)(2,1)}, u32[]{:S(2)}) copy-start(bf16[2,128,640]{2,1,0:T(8,128)(2,1)} %param.11) | copy-start | bytes 983044
  173.9 6.3 copy-start.18
  182.3 16.6 %all-to-all-start.4 = ((bf16[128,4,512]{2,1,0:T(4,128)(2,1)}), bf16[128,4,512]{2,1,0:T(4,128)(2,1)}, u32[]{:S(2)}, u32[]{:S(2)}) async-start(bf16[128,4,512]{2,1,0:T(4,128)(2,1)} %copy.249), calls=%async_computation.4 | async-start | bytes 1048576 | tf_op jit(solution)/shard_map/all_to_all | solution.py:43
  198.9 16.6 %all-to-all-start.5 = ((bf16[128,4,512]{2,1,0:T(4,128)(2,1)}), bf16[128,4,512]{2,1,0:T(4,128)(2,1)}, u32[]{:S(2)}, u32[]{:S(2)}) async-start(bf16[128,4,512]{2,1,0:T(4,128)(2,1)} %copy.252), calls=%async_computation.5 | async-start | bytes 1048576 | tf_op jit(solution)/shard_map/all_to_all | solution.py:42
  204.2 120.3 %reduce-scatter.3.cloned.1.call-start = ((), (), s32[]{:S(2)}) async-start(), calls=%async_computation.19 | async-start | bytes 4718592 | tf_op jit(solution)/shard_map/reduce_scatter | solution.py:92
  207.8 24.4 %copy-start.7 = (bf16[8,64,512]{2,1,0:T(8,128)(2,1)}, bf16[8,64,512]{2,1,0:T(8,128)(2,1)S(1)}, u32[]{:S(2)}) copy-start(bf16[8,64,512]{2,1,0:T(8,128)(2,1)S(1)} %all_to_all.173) | copy-start | bytes 1572868
  324.5 18.4 %all-to-all-start.6 = ((bf16[8,64,512]{2,0,1:T(8,128)(2,1)}), bf16[8,64,512]{2,0,1:T(8,128)(2,1)S(1)}, u32[]{:S(2)}, u32[]{:S(2)}) async-start(bf16[8,64,512]{2,0,1:T(8,128)(2,1)} %bitcast.300), calls=%async_computation.7 | async-start | bytes 1048576 | tf_op jit(solution)/shard_map/all_to_all | solution.py:48
  331.8 123.4 %all-gather.5.cloned.1.call-start = ((), (), s32[]{:S(2)}) async-start(), calls=%async_computation.20 | async-start | bytes 4718592 | tf_op jit(solution)/shard_map/all_gather | solution.py:109
  459.5 18.6 %all-to-all-start.10 = ((bf16[8,64,512]{2,0,1:T(8,128)(2,1)}), bf16[8,64,512]{2,0,1:T(8,128)(2,1)}, u32[]{:S(2)}, u32[]{:S(2)}) async-start(bf16[8,64,512]{2,0,1:T(8,128)(2,1)} %copy.269), calls=%async_computation.11 | async-start | bytes 1048576 | tf_op jit(solution)/shard_map/all_to_all | solution.py:58
  478.1 16.6 %all-to-all-start.11 = ((bf16[8,64,512]{2,0,1:T(8,128)(2,1)}), bf16[8,64,512]{2,0,1:T(8,128)(2,1)}, u32[]{:S(2)}, u32[]{:S(2)}) async-start(bf16[8,64,512]{2,0,1:T(8,128)(2,1)} %copy.273), calls=%async_computation.12 | async-start | bytes 1048576 | tf_op jit(solution)/shard_map/all_to_all | solution.py:57
  483.4 160.5 %reduce-scatter.5.cloned.1.call-start = ((), (), s32[]{:S(2)}) async-start(), calls=%async_computation.21 | async-start | bytes 4718592 | tf_op jit(solution)/shard_map/reduce_scatter | solution.py:133
  509.6 5.7 copy-start.17
  536.9 8.1 copy-start.13
  546.2 17.1 %all-to-all-start.7 = ((bf16[128,4,512]{2,1,0:T(4,128)(2,1)}), bf16[128,4,512]{2,1,0:T(4,128)(2,1)}, u32[]{:S(2)}, u32[]{:S(2)}) async-start(bf16[128,4,512]{2,1,0:T(4,128)(2,1)} %copy.258), calls=%async_computation.8 | async-start | bytes 1048576 | tf_op jit(solution)/shard_map/all_to_all | solution.py:150
  552.1 16.3 %copy-start.5 = (bf16[8,64,512]{2,0,1:T(8,128)(2,1)S(1)}, bf16[8,64,512]{2,0,1:T(8,128)(2,1)}, u32[]{:S(2)}) copy-start(bf16[8,64,512]{2,0,1:T(8,128)(2,1)} %copy-done.3) | copy-start | bytes 1572868
  555.9 12.5 %copy-start.26 = (f32[128]{0:T(128)S(1)}, f32[128]{0:T(128)}, u32[]{:S(2)}) copy-start(f32[128]{0:T(128)} %get-tuple-element.69) | copy-start | bytes 1540
  556.7 15.4 %copy-start.24 = (f32[128]{0:T(128)S(1)}, f32[128]{0:T(128)}, u32[]{:S(2)}) copy-start(f32[128]{0:T(128)} %copy-done.22) | copy-start | bytes 1540
  563.2 16.7 %all-to-all-start.14 = ((bf16[8,64,512]{2,0,1:T(8,128)(2,1)}), bf16[8,64,512]{2,0,1:T(8,128)(2,1)S(1)}, u32[]{:S(2)}, u32[]{:S(2)}) async-start(bf16[8,64,512]{2,0,1:T(8,128)(2,1)} %copy.288), calls=%async_computation.16 | async-start | bytes 1048576 | tf_op jit(solution)/shard_map/all_to_all | solution.py:57
  572.1 79.6 %copy-start.30 = (f32[128]{0:T(128)S(1)}, f32[128]{0:T(128)}, u32[]{:S(2)}) copy-start(f32[128]{0:T(128)} %get-tuple-element.26) | copy-start | bytes 1540
  572.1 79.6 %copy-start.31 = (f32[128]{0:T(128)S(1)}, f32[128]{0:T(128)}, u32[]{:S(2)}) copy-start(f32[128]{0:T(128)} %get-tuple-element.24) | copy-start | bytes 1540
  572.1 79.6 %copy-start.20 = (f32[1,128,128]{2,1,0:T(8,128)S(1)}, f32[1,128,128]{2,1,0:T(8,128)}, u32[]{:S(2)}) copy-start(f32[1,128,128]{2,1,0:T(8,128)} %convolution_bitcast_fusion.6) | copy-start | bytes 196612
  572.1 79.6 %copy-start.21 = (f32[1,128,128]{2,1,0:T(8,128)S(1)}, f32[1,128,128]{2,1,0:T(8,128)}, u32[]{:S(2)}) copy-start(f32[1,128,128]{2,1,0:T(8,128)} %convolution_bitcast_fusion.7) | copy-start | bytes 196612
  643.8 18.8 %all-to-all-start.13 = ((bf16[8,64,512]{2,0,1:T(8,128)(2,1)}), bf16[8,64,512]{2,0,1:T(8,128)(2,1)S(1)}, u32[]{:S(2)}, u32[]{:S(2)}) async-start(bf16[8,64,512]{2,0,1:T(8,128)(2,1)} %bitcast.299), calls=%async_computation.15 | async-start | bytes 1048576 | tf_op jit(solution)/shard_map/all_to_all | solution.py:58
  651.5 171.9 %all-reduce.14.cloned.1.call-start = ((), (), s32[]{:S(2)}) async-start(), calls=%async_computation.22 | async-start | bytes 1572864 | tf_op jit(solution)/shard_map/psum | solution.py:153
  676.3 9.4 %copy-start.29 = (f32[128]{0:T(128)S(1)}, f32[128]{0:T(128)}, u32[]{:S(2)}) copy-start(f32[128]{0:T(128)} %get-tuple-element.30) | copy-start | bytes 1540
  681.1 145.8 %all-to-all-start.15 = ((bf16[128,4,512]{2,1,0:T(4,128)(2,1)}), bf16[128,4,512]{2,1,0:T(4,128)(2,1)S(1)}, u32[]{:S(2)}, u32[]{:S(2)}) async-start(bf16[128,4,512]{2,1,0:T(4,128)(2,1)} %copy.295), calls=%async_computation.17 | async-start | bytes 1048576 | tf_op jit(solution)/shard_map/all_to_all | solution.py:151
  (28 other events, 106.6 us)
Sparse Core Ops, SparseCore 0:
  52.3 93.4 all-gather.2
  232.4 92.1 reduce-scatter.2
  366.5 88.6 all-gather.4
  545.1 98.6 reduce-scatter.4
  678.7 144.6 all-reduce.13
where the time goes:
time: 844 us; the launch traced here: 835 us
  waiting for transfers between devices  443 us (52%)
  blocking collectives  141 us (17%)
  starting transfers between devices  70.6 us (8%)
  local copies, waits for them, and re-layouts  69.7 us (8%)
  matrix products  61.7 us (7%)
  other arithmetic  34.1 us (4%)
  between operations  14.8 us (2%)
    all_gather x1, waiting for transfers between devices, local(): portion = lax.all_gather(dmix_one_a, 'row', axis=1, tiled=True)  88.8 us
    all_gather x1, waiting for transfers between devices, local(): lax.all_gather(right_a, 'row', axis=1, tiled=True)  77.6 us
    reduce_scatter x1, waiting for transfers between devices, local(): lax.psum_scatter(jnp.einsum('hki,hkj->ihj', columns, right_b, preferred_e...  75.3 us
    psum x1, waiting for transfers between devices, local(): lax.psum((jnp.stack([dgi_zero, dgi_one]), jnp.stack([dwi_zero, dwi_one]),...  71.4 us
    psum x1, blocking collectives, local(): lax.psum((jnp.stack([dgi_zero, dgi_one]), jnp.stack([dwi_zero, dwi_one]),...  65.7 us
    reduce_scatter x1, waiting for transfers between devices, local(): lax.psum_scatter(jnp.einsum('hij,hik->jhk', columns, left_a, preferred_el...  63.8 us
    all_to_all x2, blocking collectives, from_rows(): lax.all_to_all(cotangent, 'chan', split_axis=0, concat_axis=1, tiled=True)  29.9 us
    dot_general x6, matrix products, finish(): update = jnp.einsum('hc,hij->cij', weight, normed, precision=highest)  21.4 us
  transfers between devices with their start and end apart: 16, of which 15 were waited for; matrix products, arithmetic and copies ran while one was open for 7% of the time, Pallas kernels for 0%

commit v1 on v0

v1 whole, which is shorter than its diff:
```python
from functools import partial

import jax
import jax.numpy as jnp
from jax import lax
from jax.sharding import PartitionSpec as P

epsilon = 1e-05


def normalize(values, gain_vec):
    center = values - jnp.mean(values, axis=0, keepdims=True)
    spread = jnp.mean(center * center, axis=0, keepdims=True)
    return center * lax.rsqrt(spread + epsilon) * gain_vec[:, None, None]


def prepare(pair_f32, gain_vec, weight, mask_f):
    hidden_w = (weight.shape[1] - pair_f32.shape[0]) // 4
    normed = normalize(pair_f32, gain_vec)
    project = jnp.einsum("cd,cij->dij", weight, normed)
    left_proj = (
        mask_f * jax.nn.sigmoid(project[hidden_w : 2 * hidden_w]) * project[:hidden_w]
    ).astype(jnp.bfloat16)
    right_proj = (
        mask_f
        * jax.nn.sigmoid(project[3 * hidden_w : 4 * hidden_w])
        * project[2 * hidden_w : 3 * hidden_w]
    ).astype(jnp.bfloat16)
    gate_bf = jax.nn.sigmoid(project[4 * hidden_w :]).astype(jnp.bfloat16)
    return (left_proj, right_proj, gate_bf)


def finish(pair_f32, mixture, gate_bf, gain_vec, weight):
    normed = normalize(mixture.astype(jnp.float32), gain_vec)
    update = jnp.einsum("hc,hij->cij", weight, normed)
    return (pair_f32 + gate_bf.astype(jnp.float32) * update).astype(jnp.bfloat16)


AXES = ("row", "chan")
ROWS = 16
COLS = 128


def to_cells(field):
    channels, rows, cols = field.shape
    tiles = field.reshape(channels, rows // ROWS, ROWS, cols // COLS, COLS).transpose(1, 3, 0, 2, 4)
    tiles = tiles.reshape(-1, ROWS, COLS)
    return lax.all_to_all(tiles, "chan", split_axis=0, concat_axis=0, tiled=True)


def from_cells(cells, rows, cols):
    tiles = lax.all_to_all(cells, "chan", split_axis=0, concat_axis=0, tiled=True)
    tiles = tiles.reshape(rows // ROWS, cols // COLS, -1, ROWS, COLS).transpose(2, 0, 3, 1, 4)
    return tiles.reshape(-1, rows, cols)


def to_hidden(cells, size):
    tiles = lax.all_to_all(cells, AXES, split_axis=0, concat_axis=0, tiled=True)
    tiles = tiles.reshape(size // ROWS, size // COLS, ROWS, COLS).transpose(0, 2, 1, 3)
    return tiles.reshape(size, size)


def to_tiles(matrix):
    size = matrix.shape[0]
    tiles = matrix.astype(jnp.bfloat16).reshape(size // ROWS, ROWS, size // COLS, COLS)
    tiles = tiles.transpose(0, 2, 1, 3).reshape(-1, ROWS, COLS)
    return lax.all_to_all(tiles, AXES, split_axis=0, concat_axis=0, tiled=True)


def mul(spec, a, b):
    return jnp.einsum(spec, a, b, preferred_element_type=jnp.float32)


def sum_all(values):
    flat = jnp.concatenate([v.reshape(-1) for v in values])
    parts = lax.all_to_all(flat.reshape(128, -1), AXES, split_axis=0, concat_axis=0, tiled=True)
    total = lax.all_gather(jnp.sum(parts, axis=0), AXES, axis=0, tiled=True)
    out, at = [], 0
    for v in values:
        out.append(total[at : at + v.size].reshape(v.shape))
        at += v.size
    return out


def local(pair, grad_out, residue_chain, gain_in, w_in, gain_mid, w_out):
    size = pair.shape[2]
    group = lax.axis_index("chan")
    first_row = lax.axis_index("row") * pair.shape[1] + (group // 4) * ROWS
    first_col = (group % 4) * COLS
    validity = (residue_chain > 0).astype(jnp.float32)
    mask_f = (
        lax.dynamic_slice_in_dim(validity, first_row, ROWS)[:, None]
        * lax.dynamic_slice_in_dim(validity, first_col, COLS)[None, :]
    )
    weights_in = w_in.astype(jnp.float32)
    weights_out = w_out.astype(jnp.float32)
    prepare_masked = partial(prepare, mask_f=mask_f)
    pair_zero = to_cells(pair).astype(jnp.float32)
    cotangent = to_cells(grad_out)
    left_zero, right_zero, gate_zero = prepare_masked(pair_zero, gain_in[0], weights_in[0])
    left_a, right_a = to_hidden(left_zero, size), to_hidden(right_zero, size)
    mix_zero = to_tiles(mul("ik,jk->ij", left_a, right_a))
    field_one = finish(pair_zero, mix_zero, gate_zero, gain_mid[0], weights_out[0])
    pair_one = field_one.astype(jnp.float32)
    left_one, right_one, gate_one = prepare_masked(pair_one, gain_in[1], weights_in[1])
    left_b, right_b = to_hidden(left_one, size), to_hidden(right_one, size)
    mix_one = to_tiles(mul("ki,kj->ij", left_b, right_b))
    field_two = finish(pair_one, mix_one, gate_one, gain_mid[1], weights_out[1])
    _, pull_finish_one = jax.vjp(
        finish, pair_one, mix_one, gate_one, gain_mid[1], weights_out[1]
    )
    dfield_fin1, dmix_one, dgate_one, dgm_one, dwo_one = pull_finish_one(cotangent)
    dmix_b = to_hidden(dmix_one, size)
    dleft_one = to_tiles(mul("kj,ij->ki", right_b, dmix_b))
    dright_one = to_tiles(mul("ki,ij->kj", left_b, dmix_b))
    _, pull_prepare_one = jax.vjp(prepare_masked, pair_one, gain_in[1], weights_in[1])
    dfield_pre1, dgi_one, dwi_one = pull_prepare_one((dleft_one, dright_one, dgate_one))
    grad_field_one = (dfield_fin1 + dfield_pre1).astype(jnp.bfloat16)
    _, pull_finish_zero = jax.vjp(
        finish, pair_zero, mix_zero, gate_zero, gain_mid[0], weights_out[0]
    )
    dfield_fin0, dmix_zero, dgate_zero, dgm_zero, dwo_zero = pull_finish_zero(grad_field_one)
    dmix_a = to_hidden(dmix_zero, size)
    dleft_zero = to_tiles(mul("ij,jk->ik", dmix_a, right_a))
    dright_zero = to_tiles(mul("ij,ik->jk", dmix_a, left_a))
    _, pull_prepare_zero = jax.vjp(prepare_masked, pair_zero, gain_in[0], weights_in[0])
    dfield_pre0, dgi_zero, dwi_zero = pull_prepare_zero((dleft_zero, dright_zero, dgate_zero))
    grad_field_zero = (dfield_fin0 + dfield_pre0).astype(jnp.bfloat16)
    pair_out = from_cells(field_two, pair.shape[1], size)
    grad_pair = from_cells(grad_field_zero, pair.shape[1], size)
    summed = sum_all(
        (
            jnp.stack([dgi_zero, dgi_one]),
            jnp.stack([dwi_zero, dwi_one]),
            jnp.stack([dgm_zero, dgm_one]),
            jnp.stack([dwo_zero, dwo_one]),
        )
    )
    factor = 1.0 / size
    return (pair_out, grad_pair) + tuple(v * factor for v in summed)


def solution(mesh):
    return jax.shard_map(
        local,
        mesh=mesh,
        in_specs=(P("chan", "row", None), P("chan", "row", None), P(), P(), P(), P(), P()),
        out_specs=(P("chan", "row", None), P("chan", "row", None), P(), P(), P(), P()),
        check_vma=False,
    )
```

time: 844 us -> 539 us (0.64)
  waiting for transfers between devices: 443 us -> 297 us
  blocking collectives: 141 us -> 17.6 us
  matrix products: 61.7 us -> 32.1 us
  local copies, waits for them, and re-layouts: 69.7 us -> 51.4 us
  starting transfers between devices: 70.6 us -> 85.5 us
    all_gather x2 -> x0, waiting for transfers between devices: 166 us -> none  [the longest x1 88.8 us: local(): portion = lax.all_gather(dmix_one_a, 'row', axis=1, tiled=True)]
    reduce_scatter x2 -> x0, waiting for transfers between devices: 139 us -> none  [the longest x1 75.3 us: local(): lax.psum_scatter(jnp.einsum('hki,hkj->ihj', columns, right_b, preferred_e...]
    unnamed x5 -> x2, waiting for transfers between devices: 0.08 us -> 138 us
    all_to_all x11 -> x16, waiting for transfers between devices: 65.6 us -> 159 us  [the longest x6 63.7 us: to_tiles(): return lax.all_to_all(tiles, AXES, split_axis=0, concat_axis=0, tiled=True)]
    psum x1 -> x0, waiting for transfers between devices: 71.4 us -> none  [local(): lax.psum((jnp.stack([dgi_zero, dgi_one]), jnp.stack([dwi_zero, dwi_one]),...]
    psum x1 -> x0, blocking collectives: 65.7 us -> none  [local(): lax.psum((jnp.stack([dgi_zero, dgi_one]), jnp.stack([dwi_zero, dwi_one]),...]
    all_to_all x5 -> x1, blocking collectives: 75.5 us -> 17.6 us  [to_hidden(): tiles = lax.all_to_all(cells, AXES, split_axis=0, concat_axis=0, tiled=True)]
    dot_general x18, matrix products: 61.7 us -> 32.1 us  [the longest x6 14.5 us: finish(): update = jnp.einsum('hc,hij->cij', weight, normed)]
  transfers between devices with their start and end apart: 16 -> 17, of which waited for: 15 -> 16; matrix products, arithmetic and copies ran while one was open for 7% -> 10% of each run, Pallas kernels for 0% -> 0%
where the time goes in v1:
time: 539 us; the launch traced here: 528 us
  waiting for transfers between devices  297 us (55%)
  starting transfers between devices  85.5 us (16%)
  local copies, waits for them, and re-layouts  51.4 us (10%)
  matrix products  32.1 us (6%)
  other arithmetic  29.2 us (5%)
  blocking collectives  17.6 us (3%)
  between operations  15.3 us (3%)
    unnamed x2, waiting for transfers between devices  138 us
    all_to_all x6, waiting for transfers between devices, to_tiles(): return lax.all_to_all(tiles, AXES, split_axis=0, concat_axis=0, tiled=True)  63.7 us
    all_to_all x5, waiting for transfers between devices, to_hidden(): tiles = lax.all_to_all(cells, AXES, split_axis=0, concat_axis=0, tiled=True)  59.1 us
    all_to_all x6, starting transfers between devices, to_tiles(): return lax.all_to_all(tiles, AXES, split_axis=0, concat_axis=0, tiled=True)  29.3 us
    all_to_all x5, starting transfers between devices, to_hidden(): tiles = lax.all_to_all(cells, AXES, split_axis=0, concat_axis=0, tiled=True)  26.5 us
    all_to_all x1, blocking collectives, to_hidden(): tiles = lax.all_to_all(cells, AXES, split_axis=0, concat_axis=0, tiled=True)  17.6 us
    all_to_all x2, waiting for transfers between devices, to_cells(): lax.all_to_all(tiles, 'chan', split_axis=0, concat_axis=0, tiled=True)  16.3 us
    dot_general x6, matrix products, finish(): update = jnp.einsum('hc,hij->cij', weight, normed)  14.5 us
  transfers between devices with their start and end apart: 17, of which 16 were waited for; matrix products, arithmetic and copies ran while one was open for 10% of the time, Pallas kernels for 0%

profile of v1, /device:TPU:1, one launch (start us, length us, event | category | flops | bytes accessed | tf_op | source)
XLA Modules:
  0.0 528.2 jit_solution(6923007232506227205)
XLA Ops:
  9.3 8.4 %all-to-all-start = ((bf16[128,16,128]{2,1,0:T(8,128)(2,1)}), bf16[128,16,128]{2,1,0:T(8,128)(2,1)S(1)}, u32[]{:S(2)}, u32[]{:S(2)}) async-start(bf16[128,16,128]{2,1,0:T(8,128)(2,1)} %bitcast.1), calls=%async_computation | async-start | bytes 1048576 | tf_op jit(solution)/shard_map/all_to_all | solution.py:48
  19.4 9.5 %all-to-all-done = bf16[128,16,128]{2,1,0:T(8,128)(2,1)S(1)} async-done(((bf16[128,16,128]{2,1,0:T(8,128)(2,1)}), bf16[128,16,128]{2,1,0:T(8,128)(2,1)S(1)}, u32[]{:S(2)}, u32[]{:S(2)}) %all-to-all-start) | async-done | bytes 524320 | tf_op jit(solution)/shard_map/all_to_all | solution.py:48
  35.4 6.9 %all-to-all-start.1 = ((bf16[128,16,128]{2,1,0:T(8,128)(2,1)}), bf16[128,16,128]{2,1,0:T(8,128)(2,1)S(1)}, u32[]{:S(2)}, u32[]{:S(2)}) async-start(bf16[128,16,128]{2,1,0:T(8,128)(2,1)} %copy.125), calls=%async_computation.1 | async-start | bytes 1048576 | tf_op jit(solution)/shard_map/all_to_all | solution.py:58
  43.5 12.3 %all-to-all-done.1 = bf16[128,16,128]{2,1,0:T(8,128)(2,1)S(1)} async-done(((bf16[128,16,128]{2,1,0:T(8,128)(2,1)}), bf16[128,16,128]{2,1,0:T(8,128)(2,1)S(1)}, u32[]{:S(2)}, u32[]{:S(2)}) %all-to-all-start.1) | async-done | bytes 524320 | tf_op jit(solution)/shard_map/all_to_all | solution.py:58
  55.8 4.6 all-to-all-start.2
  60.6 13.4 %all-to-all-done.2 = bf16[128,16,128]{2,1,0:T(8,128)(2,1)S(1)} async-done(((bf16[128,16,128]{2,1,0:T(8,128)(2,1)}), bf16[128,16,128]{2,1,0:T(8,128)(2,1)S(1)}, u32[]{:S(2)}, u32[]{:S(2)}) %all-to-all-start.2) | async-done | bytes 524320 | tf_op jit(solution)/shard_map/all_to_all | solution.py:58
  75.8 4.6 all-to-all-start.3
  80.4 13.6 %all-to-all-done.3 = bf16[128,16,128]{2,1,0:T(8,128)(2,1)S(1)} async-done(((bf16[128,16,128]{2,1,0:T(8,128)(2,1)}), bf16[128,16,128]{2,1,0:T(8,128)(2,1)S(1)}, u32[]{:S(2)}, u32[]{:S(2)}) %all-to-all-start.3) | async-done | bytes 524320 | tf_op jit(solution)/shard_map/all_to_all | solution.py:67
  103.0 4.6 all-to-all-start.4
  108.7 12.5 %all-to-all-done.4 = bf16[128,16,128]{2,1,0:T(8,128)(2,1)S(1)} async-done(((bf16[128,16,128]{2,1,0:T(8,128)(2,1)}), bf16[128,16,128]{2,1,0:T(8,128)(2,1)S(1)}, u32[]{:S(2)}, u32[]{:S(2)}) %all-to-all-start.4) | async-done | bytes 524320 | tf_op jit(solution)/shard_map/all_to_all | solution.py:58
  121.2 5.0 all-to-all-start.5
  128.3 11.6 %all-to-all-done.5 = bf16[128,16,128]{2,1,0:T(8,128)(2,1)S(1)} async-done(((bf16[128,16,128]{2,1,0:T(8,128)(2,1)}), bf16[128,16,128]{2,1,0:T(8,128)(2,1)S(1)}, u32[]{:S(2)}, u32[]{:S(2)}) %all-to-all-start.5) | async-done | bytes 524320 | tf_op jit(solution)/shard_map/all_to_all | solution.py:58
  148.8 6.8 %all-to-all-done.8 = bf16[128,16,128]{2,1,0:T(8,128)(2,1)S(1)} async-done(((bf16[128,16,128]{2,1,0:T(8,128)(2,1)}), bf16[128,16,128]{2,1,0:T(8,128)(2,1)S(1)}, u32[]{:S(2)}, u32[]{:S(2)}) %all-to-all-start.8) | async-done | bytes 524320 | tf_op jit(solution)/shard_map/all_to_all | solution.py:48
  155.6 4.8 all-to-all-start.6
  160.9 13.2 %all-to-all-done.6 = bf16[128,16,128]{2,1,0:T(8,128)(2,1)S(1)} async-done(((bf16[128,16,128]{2,1,0:T(8,128)(2,1)}), bf16[128,16,128]{2,1,0:T(8,128)(2,1)S(1)}, u32[]{:S(2)}, u32[]{:S(2)}) %all-to-all-start.6) | async-done | bytes 524320 | tf_op jit(solution)/shard_map/all_to_all | solution.py:67
  179.6 17.6 %all_to_all.90 = bf16[128,16,128]{2,1,0:T(8,128)(2,1)S(1)} all-to-all(bf16[128,16,128]{2,1,0:T(8,128)(2,1)S(1)} %copy.145), channel_id=1, replica_groups=mesh['row'=8,'chan'=16] {'row','chan'}, dimensions={0} | all-to-all | bytes 1048576 | tf_op jit(solution)/shard_map/all_to_all | solution.py:58
  201.6 4.6 all-to-all-start.11
  212.5 7.3 %all-to-all-done.11 = bf16[128,16,128]{2,1,0:T(8,128)(2,1)S(1)} async-done(((bf16[128,16,128]{2,1,0:T(8,128)(2,1)}), bf16[128,16,128]{2,1,0:T(8,128)(2,1)S(1)}, u32[]{:S(2)}, u32[]{:S(2)}) %all-to-all-start.11) | async-done | bytes 524320 | tf_op jit(solution)/shard_map/all_to_all | solution.py:67
  219.8 6.0 %all-to-all-start.10 = ((bf16[128,16,128]{2,1,0:T(8,128)(2,1)}), bf16[128,16,128]{2,1,0:T(8,128)(2,1)}, u32[]{:S(2)}, u32[]{:S(2)}) async-start(bf16[128,16,128]{2,1,0:T(8,128)(2,1)} %bitcast.180), calls=%async_computation.10 | async-start | bytes 1048576 | tf_op jit(solution)/shard_map/all_to_all | solution.py:67
  227.0 12.0 %all-to-all-done.10 = bf16[128,16,128]{2,1,0:T(8,128)(2,1)} async-done(((bf16[128,16,128]{2,1,0:T(8,128)(2,1)}), bf16[128,16,128]{2,1,0:T(8,128)(2,1)}, u32[]{:S(2)}, u32[]{:S(2)}) %all-to-all-start.10) | async-done | bytes 524320 | tf_op jit(solution)/shard_map/all_to_all | solution.py:67
  240.5 4.6 fusion.72
  257.2 5.5 %all-to-all-start.12 = ((bf16[128,16,128]{2,1,0:T(8,128)(2,1)}), bf16[128,16,128]{2,1,0:T(8,128)(2,1)}, u32[]{:S(2)}, u32[]{:S(2)}) async-start(bf16[128,16,128]{2,1,0:T(8,128)(2,1)} %copy.155), calls=%async_computation.12 | async-start | bytes 1048576 | tf_op jit(solution)/shard_map/all_to_all | solution.py:58
  266.7 9.3 %all-to-all-done.12 = bf16[128,16,128]{2,1,0:T(8,128)(2,1)} async-done(((bf16[128,16,128]{2,1,0:T(8,128)(2,1)}), bf16[128,16,128]{2,1,0:T(8,128)(2,1)}, u32[]{:S(2)}, u32[]{:S(2)}) %all-to-all-start.12) | async-done | bytes 524320 | tf_op jit(solution)/shard_map/all_to_all | solution.py:58
  282.5 4.6 all-to-all-start.14
  292.3 8.4 %all-to-all-done.14 = bf16[128,16,128]{2,1,0:T(8,128)(2,1)S(1)} async-done(((bf16[128,16,128]{2,1,0:T(8,128)(2,1)}), bf16[128,16,128]{2,1,0:T(8,128)(2,1)S(1)}, u32[]{:S(2)}, u32[]{:S(2)}) %all-to-all-start.14) | async-done | bytes 524320 | tf_op jit(solution)/shard_map/all_to_all | solution.py:67
  300.7 4.9 all-to-all-start.13
  310.1 9.1 %all-to-all-done.13 = bf16[128,16,128]{2,1,0:T(8,128)(2,1)S(1)} async-done(((bf16[128,16,128]{2,1,0:T(8,128)(2,1)}), bf16[128,16,128]{2,1,0:T(8,128)(2,1)S(1)}, u32[]{:S(2)}, u32[]{:S(2)}) %all-to-all-start.13) | async-done | bytes 524320 | tf_op jit(solution)/shard_map/all_to_all | solution.py:67
  319.2 5.1 all-to-all-start.7
  336.9 7.2 %all-to-all-start.16 = ((f32[128,1,1540]{2,1,0:T(1,128)}), f32[128,1,1540]{2,1,0:T(1,128)S(1)}, u32[]{:S(2)}, u32[]{:S(2)}) async-start(f32[128,1,1540]{2,1,0:T(1,128)} %all_to_all.72), calls=%async_computation.16 | async-start | bytes 1703936 | tf_op jit(solution)/shard_map/all_to_all | solution.py:76
  348.0 13.1 %all-to-all-done.16 = f32[128,1,1540]{2,1,0:T(1,128)S(1)} async-done(((f32[128,1,1540]{2,1,0:T(1,128)}), f32[128,1,1540]{2,1,0:T(1,128)S(1)}, u32[]{:S(2)}, u32[]{:S(2)}) %all-to-all-start.16) | async-done | bytes 788512 | tf_op jit(solution)/shard_map/all_to_all | solution.py:76
  369.9 6.9 %all-to-all-done.15 = bf16[128,16,128]{2,1,0:T(8,128)(2,1)S(1)} async-done(((bf16[128,16,128]{2,1,0:T(8,128)(2,1)}), bf16[128,16,128]{2,1,0:T(8,128)(2,1)S(1)}, u32[]{:S(2)}, u32[]{:S(2)}) %all-to-all-start.15) | async-done | bytes 524320 | tf_op jit(solution)/shard_map/all_to_all | solution.py:52
  378.2 138.0 %all-reduce.13.cloned.1.call-done = f32[197120]{0:T(1024)} async-done(((f32[197120]{0:T(1024)}), f32[197120]{0:T(1024)}) %all-reduce.13.cloned.1.call-update) | async-done | bytes 788496
  (215 shorter events, 117.3 us)
Async XLA Ops:
  7.2 23.1 %copy-start.14 = (bf16[2,128,640]{2,1,0:T(8,128)(2,1)S(1)}, bf16[2,128,640]{2,1,0:T(8,128)(2,1)}, u32[]{:S(2)}) copy-start(bf16[2,128,640]{2,1,0:T(8,128)(2,1)} %param.11) | copy-start | bytes 983044
  9.3 19.6 %all-to-all-start = ((bf16[128,16,128]{2,1,0:T(8,128)(2,1)}), bf16[128,16,128]{2,1,0:T(8,128)(2,1)S(1)}, u32[]{:S(2)}, u32[]{:S(2)}) async-start(bf16[128,16,128]{2,1,0:T(8,128)(2,1)} %bitcast.1), calls=%async_computation | async-start | bytes 1048576 | tf_op jit(solution)/shard_map/all_to_all | solution.py:48
  19.3 228.1 %copy-start.36 = (f32[128]{0:T(128)}, f32[128]{0:T(128)S(1)}, u32[]{:S(2)}) copy-start(f32[128]{0:T(128)S(1)} %get-tuple-element.46) | copy-start | bytes 1540
  19.4 221.1 %copy-start.24 = (f32[16,128]{1,0:T(8,128)}, f32[16,128]{1,0:T(8,128)S(1)}, u32[]{:S(2)}) copy-start(f32[16,128]{1,0:T(8,128)S(1)} %broadcast_multiply_fusion) | copy-start | bytes 24580
  35.4 45.0 %copy-start.43 = (f32[2,128]{1,0:T(2,128)S(1)}, f32[2,128]{1,0:T(2,128)}, u32[]{:S(2)}) copy-start(f32[2,128]{1,0:T(2,128)} %param.12) | copy-start | bytes 3076
  35.4 20.4 %all-to-all-start.1 = ((bf16[128,16,128]{2,1,0:T(8,128)(2,1)}), bf16[128,16,128]{2,1,0:T(8,128)(2,1)S(1)}, u32[]{:S(2)}, u32[]{:S(2)}) async-start(bf16[128,16,128]{2,1,0:T(8,128)(2,1)} %copy.125), calls=%async_computation.1 | async-start | bytes 1048576 | tf_op jit(solution)/shard_map/all_to_all | solution.py:58
  42.3 52.1 %copy-start.44 = (bf16[2,128,128]{2,1,0:T(8,128)(2,1)S(1)}, bf16[2,128,128]{2,1,0:T(8,128)(2,1)}, u32[]{:S(2)}) copy-start(bf16[2,128,128]{2,1,0:T(8,128)(2,1)} %param.13) | copy-start | bytes 196612
  55.8 18.2 %all-to-all-start.2 = ((bf16[128,16,128]{2,1,0:T(8,128)(2,1)}), bf16[128,16,128]{2,1,0:T(8,128)(2,1)S(1)}, u32[]{:S(2)}, u32[]{:S(2)}) async-start(bf16[128,16,128]{2,1,0:T(8,128)(2,1)} %copy.127), calls=%async_computation.2 | async-start | bytes 1048576 | tf_op jit(solution)/shard_map/all_to_all | solution.py:58
  60.6 36.5 %copy-start.5 = (bf16[32,16,4,128]{3,2,1,0:T(4,128)(2,1)}, bf16[32,16,4,128]{3,2,1,0:T(4,128)(2,1)S(1)}, u32[]{:S(2)}) copy-start(bf16[32,16,4,128]{3,2,1,0:T(4,128)(2,1)S(1)} %copy.126) | copy-start | bytes 1572868
  74.3 20.1 %copy-start.7 = (bf16[32,16,4,128]{3,2,1,0:T(4,128)(2,1)}, bf16[32,16,4,128]{3,2,1,0:T(4,128)(2,1)S(1)}, u32[]{:S(2)}) copy-start(bf16[32,16,4,128]{3,2,1,0:T(4,128)(2,1)S(1)} %copy.128) | copy-start | bytes 1572868
  75.8 18.2 %all-to-all-start.3 = ((bf16[128,16,128]{2,1,0:T(8,128)(2,1)}), bf16[128,16,128]{2,1,0:T(8,128)(2,1)S(1)}, u32[]{:S(2)}, u32[]{:S(2)}) async-start(bf16[128,16,128]{2,1,0:T(8,128)(2,1)} %bitcast.11), calls=%async_computation.3 | async-start | bytes 1048576 | tf_op jit(solution)/shard_map/all_to_all | solution.py:67
  80.4 93.8 %copy-start.40 = (f32[128]{0:T(128)}, f32[128]{0:T(128)S(1)}, u32[]{:S(2)}) copy-start(f32[128]{0:T(128)S(1)} %get-tuple-element.49) | copy-start | bytes 1540
  97.1 150.3 %copy-start.16 = (f32[16,128]{1,0:T(8,128)}, f32[16,128]{1,0:T(8,128)S(1)}, u32[]{:S(2)}) copy-start(f32[16,128]{1,0:T(8,128)S(1)} %broadcast_multiply_fusion.2) | copy-start | bytes 24580
  97.8 149.7 %copy-start.20 = (f32[16,128]{1,0:T(8,128)}, f32[16,128]{1,0:T(8,128)S(1)}, u32[]{:S(2)}) copy-start(f32[16,128]{1,0:T(8,128)S(1)} %fusion.170) | copy-start | bytes 24580
  103.0 18.2 %all-to-all-start.4 = ((bf16[128,16,128]{2,1,0:T(8,128)(2,1)}), bf16[128,16,128]{2,1,0:T(8,128)(2,1)S(1)}, u32[]{:S(2)}, u32[]{:S(2)}) async-start(bf16[128,16,128]{2,1,0:T(8,128)(2,1)} %copy.133), calls=%async_computation.4 | async-start | bytes 1048576 | tf_op jit(solution)/shard_map/all_to_all | solution.py:58
  121.2 18.7 %all-to-all-start.5 = ((bf16[128,16,128]{2,1,0:T(8,128)(2,1)}), bf16[128,16,128]{2,1,0:T(8,128)(2,1)S(1)}, u32[]{:S(2)}, u32[]{:S(2)}) async-start(bf16[128,16,128]{2,1,0:T(8,128)(2,1)} %copy.135), calls=%async_computation.5 | async-start | bytes 1048576 | tf_op jit(solution)/shard_map/all_to_all | solution.py:58
  139.9 15.7 %all-to-all-start.8 = ((bf16[128,16,128]{2,1,0:T(8,128)(2,1)}), bf16[128,16,128]{2,1,0:T(8,128)(2,1)S(1)}, u32[]{:S(2)}, u32[]{:S(2)}) async-start(bf16[128,16,128]{2,1,0:T(8,128)(2,1)} %bitcast.177), calls=%async_computation.8 | async-start | bytes 1048576 | tf_op jit(solution)/shard_map/all_to_all | solution.py:48
  155.6 18.4 %all-to-all-start.6 = ((bf16[128,16,128]{2,1,0:T(8,128)(2,1)}), bf16[128,16,128]{2,1,0:T(8,128)(2,1)S(1)}, u32[]{:S(2)}, u32[]{:S(2)}) async-start(bf16[128,16,128]{2,1,0:T(8,128)(2,1)} %bitcast.25), calls=%async_computation.6 | async-start | bytes 1048576 | tf_op jit(solution)/shard_map/all_to_all | solution.py:67
  174.2 66.3 %copy-start.28 = (f32[16,128]{1,0:T(8,128)}, f32[16,128]{1,0:T(8,128)S(1)}, u32[]{:S(2)}) copy-start(f32[16,128]{1,0:T(8,128)S(1)} %broadcast_multiply_fusion.1) | copy-start | bytes 24580
  176.1 22.2 %copy-start.10 = (bf16[32,16,4,128]{3,2,1,0:T(4,128)(2,1)S(1)}, bf16[32,16,4,128]{3,2,1,0:T(4,128)(2,1)}, u32[]{:S(2)}) copy-start(bf16[32,16,4,128]{3,2,1,0:T(4,128)(2,1)} %copy-done.9) | copy-start | bytes 1572868
  176.1 64.4 %copy-start.30 = (f32[16,128]{1,0:T(8,128)}, f32[16,128]{1,0:T(8,128)S(1)}, u32[]{:S(2)}) copy-start(f32[16,128]{1,0:T(8,128)S(1)} %get-tuple-element.45) | copy-start | bytes 24580
  199.5 41.0 %copy-start.41 = (f32[128]{0:T(128)S(1)}, f32[128]{0:T(128)}, u32[]{:S(2)}) copy-start(f32[128]{0:T(128)} %copy-done.40) | copy-start | bytes 1540
  201.6 18.2 %all-to-all-start.11 = ((bf16[128,16,128]{2,1,0:T(8,128)(2,1)}), bf16[128,16,128]{2,1,0:T(8,128)(2,1)S(1)}, u32[]{:S(2)}, u32[]{:S(2)}) async-start(bf16[128,16,128]{2,1,0:T(8,128)(2,1)} %bitcast.179), calls=%async_computation.11 | async-start | bytes 1048576 | tf_op jit(solution)/shard_map/all_to_all | solution.py:67
  219.8 19.2 %all-to-all-start.10 = ((bf16[128,16,128]{2,1,0:T(8,128)(2,1)}), bf16[128,16,128]{2,1,0:T(8,128)(2,1)}, u32[]{:S(2)}, u32[]{:S(2)}) async-start(bf16[128,16,128]{2,1,0:T(8,128)(2,1)} %bitcast.180), calls=%async_computation.10 | async-start | bytes 1048576 | tf_op jit(solution)/shard_map/all_to_all | solution.py:67
  257.2 18.8 %all-to-all-start.12 = ((bf16[128,16,128]{2,1,0:T(8,128)(2,1)}), bf16[128,16,128]{2,1,0:T(8,128)(2,1)}, u32[]{:S(2)}, u32[]{:S(2)}) async-start(bf16[128,16,128]{2,1,0:T(8,128)(2,1)} %copy.155), calls=%async_computation.12 | async-start | bytes 1048576 | tf_op jit(solution)/shard_map/all_to_all | solution.py:58
  282.5 18.2 %all-to-all-start.14 = ((bf16[128,16,128]{2,1,0:T(8,128)(2,1)}), bf16[128,16,128]{2,1,0:T(8,128)(2,1)S(1)}, u32[]{:S(2)}, u32[]{:S(2)}) async-start(bf16[128,16,128]{2,1,0:T(8,128)(2,1)} %bitcast.49), calls=%async_computation.14 | async-start | bytes 1048576 | tf_op jit(solution)/shard_map/all_to_all | solution.py:67
  287.1 19.2 %copy-start.17 = (f32[16,128]{1,0:T(8,128)S(1)}, f32[16,128]{1,0:T(8,128)}, u32[]{:S(2)}) copy-start(f32[16,128]{1,0:T(8,128)} %copy-done.16) | copy-start | bytes 24580
  300.7 18.4 %all-to-all-start.13 = ((bf16[128,16,128]{2,1,0:T(8,128)(2,1)}), bf16[128,16,128]{2,1,0:T(8,128)(2,1)S(1)}, u32[]{:S(2)}, u32[]{:S(2)}) async-start(bf16[128,16,128]{2,1,0:T(8,128)(2,1)} %bitcast.47), calls=%async_computation.13 | async-start | bytes 1048576 | tf_op jit(solution)/shard_map/all_to_all | solution.py:67
  319.2 17.7 %all-to-all-start.7 = ((bf16[128,16,128]{2,1,0:T(8,128)(2,1)}), bf16[128,16,128]{2,1,0:T(8,128)(2,1)}, u32[]{:S(2)}, u32[]{:S(2)}) async-start(bf16[128,16,128]{2,1,0:T(8,128)(2,1)} %copy.140), calls=%async_computation.7 | async-start | bytes 1048576 | tf_op jit(solution)/shard_map/all_to_all | solution.py:52
  336.9 24.2 %all-to-all-start.16 = ((f32[128,1,1540]{2,1,0:T(1,128)}), f32[128,1,1540]{2,1,0:T(1,128)S(1)}, u32[]{:S(2)}, u32[]{:S(2)}) async-start(f32[128,1,1540]{2,1,0:T(1,128)} %all_to_all.72), calls=%async_computation.16 | async-start | bytes 1703936 | tf_op jit(solution)/shard_map/all_to_all | solution.py:76
  361.1 15.7 %all-to-all-start.15 = ((bf16[128,16,128]{2,1,0:T(8,128)(2,1)}), bf16[128,16,128]{2,1,0:T(8,128)(2,1)S(1)}, u32[]{:S(2)}, u32[]{:S(2)}) async-start(bf16[128,16,128]{2,1,0:T(8,128)(2,1)} %copy.163), calls=%async_computation.15 | async-start | bytes 1048576 | tf_op jit(solution)/shard_map/all_to_all | solution.py:52
  365.6 150.6 %all-reduce.13.cloned.1.call-start = ((), (), s32[]{:S(2)}) async-start(), calls=%async_computation.17 | async-start | bytes 1581056
  (36 other events, 199.4 us)
Sparse Core Ops, SparseCore 0:
  371.2 144.9 all-reduce.12

commit v2 on v1

--- a/solution.py
+++ b/solution.py
@@ -3,6 +3,8 @@
 import jax
 import jax.numpy as jnp
 from jax import lax
+from jax.experimental import pallas as pl
+from jax.experimental.pallas import tpu as pltpu
 from jax.sharding import PartitionSpec as P
 
 epsilon = 1e-05
@@ -36,35 +38,117 @@
     return (pair_f32 + gate_bf.astype(jnp.float32) * update).astype(jnp.bfloat16)
 
 
-AXES = ("row", "chan")
 ROWS = 16
 COLS = 128
+
+
+MESH = pl.DeviceIdType.MESH
+
+
+def exchange_kernel(axes, gather, count, *refs):
+    given, got = refs[:count], refs[count : 2 * count]
+    send, recv, own = refs[2 * count :]
+    row, chan = lax.axis_index("row"), lax.axis_index("chan")
+    groups = lax.axis_size("chan")
+    if axes == "chan":
+        members, me = groups, chan
+    else:
+        members, me = groups * lax.axis_size("row"), row * groups + chan
+
+    def place(to):
+        return (row, to) if axes == "chan" else (to // groups, lax.rem(to, groups))
+
+    barrier = pltpu.get_barrier_semaphore()
+
+    def greet(step, carry):
+        other = lax.rem(me + step, members)
+        pl.semaphore_signal(barrier, inc=1, device_id=place(other), device_id_type=MESH)
+        return carry
+
+    lax.fori_loop(1, members, greet, 0)
+    pl.semaphore_wait(barrier, members - 1)
+
+    def dispatch(step, carry):
+        other = lax.rem(me + step, members)
+        for at, (src, dst) in enumerate(zip(given, got)):
+            pltpu.make_async_remote_copy(
+                src_ref=src.at[0] if gather else src.at[other],
+                dst_ref=dst.at[me],
+                send_sem=send.at[at],
+                recv_sem=recv.at[at],
+                device_id=place(other),
+                device_id_type=MESH,
+            ).start()
+        return carry
+
+    lax.fori_loop(1, members, dispatch, 0)
+    for at, (src, dst) in enumerate(zip(given, got)):
+        keep = pltpu.make_async_copy(src.at[0] if gather else src.at[me], dst.at[me], own)
+        keep.start()
+        keep.wait()
+    for at, (src, dst) in enumerate(zip(given, got)):
+        rest = dst.at[pl.ds(0, members - 1)]
+        landed = pltpu.make_async_remote_copy(
+            src_ref=rest,
+            dst_ref=rest,
+            send_sem=send.at[at],
+            recv_sem=recv.at[at],
+            device_id=(row, chan),
+            device_id_type=MESH,
+        )
+        landed.wait_recv()
+        landed.wait_send()
+
+
+def exchange(ident, axes, *arrays, gather=False):
+    members = 16 if axes == "chan" else 128
+    count = len(arrays)
+    space = pl.BlockSpec(memory_space=pl.ANY)
+    return pl.pallas_call(
+        partial(exchange_kernel, axes, gather, count),
+        out_shape=[jax.ShapeDtypeStruct((members,) + a.shape[1:], a.dtype) for a in arrays],
+        in_specs=[space] * count,
+        out_specs=[space] * count,
+        scratch_shapes=[
+            pltpu.SemaphoreType.DMA((count,)),
+            pltpu.SemaphoreType.DMA((count,)),
+            pltpu.SemaphoreType.DMA,
+        ],
+        compiler_params=pltpu.CompilerParams(collective_id=ident, has_side_effects=True),
+    )(*arrays)
 
 
 def to_cells(field):
     channels, rows, cols = field.shape
     tiles = field.reshape(channels, rows // ROWS, ROWS, cols // COLS, COLS).transpose(1, 3, 0, 2, 4)
-    tiles = tiles.reshape(-1, ROWS, COLS)
-    return lax.all_to_all(tiles, "chan", split_axis=0, concat_axis=0, tiled=True)
+    tiles = tiles.reshape(-1, channels * ROWS, COLS)
+    return exchange(0, "chan", tiles)[0].reshape(-1, ROWS, COLS)
 
 
 def from_cells(cells, rows, cols):
-    tiles = lax.all_to_all(cells, "chan", split_axis=0, concat_axis=0, tiled=True)
+    tiles = exchange(0, "chan", cells.reshape(16, -1, COLS))[0]
     tiles = tiles.reshape(rows // ROWS, cols // COLS, -1, ROWS, COLS).transpose(2, 0, 3, 1, 4)
     return tiles.reshape(-1, rows, cols)
 
 
-def to_hidden(cells, size):
-    tiles = lax.all_to_all(cells, AXES, split_axis=0, concat_axis=0, tiled=True)
+def as_matrix(tiles, size):
     tiles = tiles.reshape(size // ROWS, size // COLS, ROWS, COLS).transpose(0, 2, 1, 3)
     return tiles.reshape(size, size)
 
 
-def to_tiles(matrix):
+def to_hidden(size, *cells):
+    moved = exchange(len(cells), "all", *cells)
+    return [as_matrix(t, size) for t in moved]
+
+
+def as_tiles(matrix):
     size = matrix.shape[0]
     tiles = matrix.astype(jnp.bfloat16).reshape(size // ROWS, ROWS, size // COLS, COLS)
-    tiles = tiles.transpose(0, 2, 1, 3).reshape(-1, ROWS, COLS)
-    return lax.all_to_all(tiles, AXES, split_axis=0, concat_axis=0, tiled=True)
+    return tiles.transpose(0, 2, 1, 3).reshape(-1, ROWS, COLS)
+
+
+def to_tiles(*matrices):
+    return exchange(len(matrices), "all", *[as_tiles(m) for m in matrices])
 
 
 def mul(spec, a, b):
@@ -73,8 +157,11 @@
 
 def sum_all(values):
     flat = jnp.concatenate([v.reshape(-1) for v in values])
-    parts = lax.all_to_all(flat.reshape(128, -1), AXES, split_axis=0, concat_axis=0, tiled=True)
-    total = lax.all_gather(jnp.sum(parts, axis=0), AXES, axis=0, tiled=True)
+    room = 128 * ROWS * COLS
+    flat = jnp.pad(flat, (0, room - flat.size)).reshape(128, ROWS, COLS)
+    parts = exchange(3, "all", flat)[0]
+    total = exchange(4, "all", jnp.sum(parts, axis=0, keepdims=True), gather=True)[0]
+    total = total.reshape(-1)
     out, at = [], 0
     for v in values:
         out.append(total[at : at + v.size].reshape(v.shape))
@@ -98,21 +185,22 @@
     pair_zero = to_cells(pair).astype(jnp.float32)
     cotangent = to_cells(grad_out)
     left_zero, right_zero, gate_zero = prepare_masked(pair_zero, gain_in[0], weights_in[0])
-    left_a, right_a = to_hidden(left_zero, size), to_hidden(right_zero, size)
-    mix_zero = to_tiles(mul("ik,jk->ij", left_a, right_a))
+    left_a, right_a = to_hidden(size, left_zero, right_zero)
+    (mix_zero,) = to_tiles(mul("ik,jk->ij", left_a, right_a))
     field_one = finish(pair_zero, mix_zero, gate_zero, gain_mid[0], weights_out[0])
     pair_one = field_one.astype(jnp.float32)
     left_one, right_one, gate_one = prepare_masked(pair_one, gain_in[1], weights_in[1])
-    left_b, right_b = to_hidden(left_one, size), to_hidden(right_one, size)
-    mix_one = to_tiles(mul("ki,kj->ij", left_b, right_b))
+    left_b, right_b = to_hidden(size, left_one, right_one)
+    (mix_one,) = to_tiles(mul("ki,kj->ij", left_b, right_b))
     field_two = finish(pair_one, mix_one, gate_one, gain_mid[1], weights_out[1])
     _, pull_finish_one = jax.vjp(
         finish, pair_one, mix_one, gate_one, gain_mid[1], weights_out[1]
     )
     dfield_fin1, dmix_one, dgate_one, dgm_one, dwo_one = pull_finish_one(cotangent)
-    dmix_b = to_hidden(dmix_one, size)
-    dleft_one = to_tiles(mul("kj,ij->ki", right_b, dmix_b))
-    dright_one = to_tiles(mul("ki,ij->kj", left_b, dmix_b))
+    (dmix_b,) = to_hidden(size, dmix_one)
+    dleft_one, dright_one = to_tiles(
+        mul("kj,ij->ki", right_b, dmix_b), mul("ki,ij->kj", left_b, dmix_b)
+    )
     _, pull_prepare_one = jax.vjp(prepare_masked, pair_one, gain_in[1], weights_in[1])
     dfield_pre1, dgi_one, dwi_one = pull_prepare_one((dleft_one, dright_one, dgate_one))
     grad_field_one = (dfield_fin1 + dfield_pre1).astype(jnp.bfloat16)
@@ -120,9 +208,10 @@
         finish, pair_zero, mix_zero, gate_zero, gain_mid[0], weights_out[0]
     )
     dfield_fin0, dmix_zero, dgate_zero, dgm_zero, dwo_zero = pull_finish_zero(grad_field_one)
-    dmix_a = to_hidden(dmix_zero, size)
-    dleft_zero = to_tiles(mul("ij,jk->ik", dmix_a, right_a))
-    dright_zero = to_tiles(mul("ij,ik->jk", dmix_a, left_a))
+    (dmix_a,) = to_hidden(size, dmix_zero)
+    dleft_zero, dright_zero = to_tiles(
+        mul("ij,jk->ik", dmix_a, right_a), mul("ij,ik->jk", dmix_a, left_a)
+    )
     _, pull_prepare_zero = jax.vjp(prepare_masked, pair_zero, gain_in[0], weights_in[0])
     dfield_pre0, dgi_zero, dwi_zero = pull_prepare_zero((dleft_zero, dright_zero, dgate_zero))
     grad_field_zero = (dfield_fin0 + dfield_pre0).astype(jnp.bfloat16)

time: 539 us -> 404 us (0.75); the launches traced: 528 us -> 402 us
  waiting for transfers between devices: 297 us -> 0 us
  Pallas kernels: 0 us -> 262 us
  starting transfers between devices: 85.5 us -> 0 us
  other arithmetic: 29.2 us -> 62.9 us
  blocking collectives: 17.6 us -> 0 us
  between operations: 15.3 us -> 1.38 us
  matrix products: 32.1 us -> 21.2 us
    pallas_call x0 -> x14, Pallas kernels: none -> 262 us  [exchange(): pl.pallas_call(partial(exchange_kernel, axes, gather, count), out_shape=[...]
    all_to_all x16 -> x0, waiting for transfers between devices: 159 us -> none  [the longest x6 63.7 us: to_tiles(): return lax.all_to_all(tiles, AXES, split_axis=0, concat_axis=0, tiled=True)]
    unnamed x2 -> x0, waiting for transfers between devices: 138 us -> none
    all_to_all x16 -> x0, starting transfers between devices: 85.5 us -> none  [the longest x6 29.3 us: to_tiles(): return lax.all_to_all(tiles, AXES, split_axis=0, concat_axis=0, tiled=True)]
    all_to_all x1 -> x0, blocking collectives: 17.6 us -> none  [to_hidden(): tiles = lax.all_to_all(cells, AXES, split_axis=0, concat_axis=0, tiled=True)]
    dot_general x6, matrix products: 14.5 us -> 1.88 us  [finish(): update = jnp.einsum('hc,hij->cij', weight, normed)]
    dot_general x0 -> x2, local copies, waits for them, and re-layouts: none -> 12.4 us  [prepare(): project = jnp.einsum('cd,cij->dij', weight, normed)]
    convert_element_type x8 -> x0, local copies, waits for them, and re-layouts: 9.67 us -> none  [the longest x2 2.38 us: prepare(): left_proj = (mask_f * jax.nn.sigmoid(project[hidden_w:2 * hidden_w]) * pr...]
  transfers between devices with their start and end apart: 17 -> 0, of which waited for: 16 -> 0; matrix products, arithmetic and copies ran while one was open for 10% -> 0% of each run, Pallas kernels for 0% -> 0%
where the time goes in v2:
time: 404 us; the launch traced here: 402 us
  Pallas kernels  262 us (65%)
  other arithmetic  62.9 us (16%)
  local copies, waits for them, and re-layouts  53.7 us (13%)
  matrix products  21.2 us (5%)
    pallas_call x14, Pallas kernels, exchange(): pl.pallas_call(partial(exchange_kernel, axes, gather, count), out_shape=[...  262 us
    reduce_sum x8, other arithmetic, normalize(): return center * lax.rsqrt(spread + epsilon) * gain_vec[:, None, None]  13 us
    dot_general x2, local copies, waits for them, and re-layouts, prepare(): project = jnp.einsum('cd,cij->dij', weight, normed)  12.4 us
    reshape x12, local copies, waits for them, and re-layouts, as_tiles(): matrix.astype(jnp.bfloat16).reshape(size // ROWS, ROWS, size // COLS, COLS)  12.1 us
    dot_general x6, matrix products, prepare(): project = jnp.einsum('cd,cij->dij', weight, normed)  11.3 us
    mul x2, other arithmetic, prepare(): gate_bf = jax.nn.sigmoid(project[4 * hidden_w:]).astype(jnp.bfloat16)  9.26 us
    reshape x6, local copies, waits for them, and re-layouts, as_matrix(): tiles.reshape(size // ROWS, size // COLS, ROWS, COLS).transpose(0, 2, 1, 3)  8.12 us

profile of v2, /device:TPU:1, one launch (start us, length us, event | category | flops | bytes accessed | tf_op | source)
XLA Modules:
  0.0 401.7 jit_solution(12944992693189187062)
XLA Ops:
  5.4 14.0 %shard_map.118 = bf16[16,128,128]{2,1,0:T(8,128)(2,1)} custom-call(bf16[16,128,128]{2,1,0:T(8,128)(2,1)} %bitcast.252), custom_call_target="tpu_custom_call" | custom-call | tf_op jit(solution)/shard_map/pallas_call | solution.py:107
  22.8 13.0 %shard_map.124 = bf16[16,128,128]{2,1,0:T(8,128)(2,1)} custom-call(bf16[16,128,128]{2,1,0:T(8,128)(2,1)} %bitcast.253), custom_call_target="tpu_custom_call" | custom-call | tf_op jit(solution)/shard_map/pallas_call | solution.py:107
  37.7 3.2 fusion.79
  40.9 6.1 %copy.53 = f32[16,128,640]{1,0,2:T(8,128)} copy(f32[16,128,640]{2,1,0:T(8,128)} %fusion.79) | data formatting | bytes 10485760 | tf_op jit(solution)/shard_map/cd,cij->dij/dot_general | solution.py:22
  47.0 3.7 multiply_convert_fusion.2
  50.7 26.3 %shard_map.119 = (bf16[128,16,128]{2,1,0:T(8,128)(2,1)}, bf16[128,16,128]{2,1,0:T(8,128)(2,1)}) custom-call(bf16[128,16,128]{2,1,0:T(8,128)(2,1)} %get-tuple-element.55.refs_0_, bf16[128,16,128]{2,1,0:T(8,128)(2,1)} %get-tuple-element.54.refs_1_), custom_call_target="tpu_custom_call" | custom-call | tf_op jit(solution)/shard_map/pallas_call | solution.py:107
  82.1 16.1 %shard_map.120 = bf16[128,16,128]{2,1,0:T(8,128)(2,1)} custom-call(bf16[128,16,128]{2,1,0:T(8,128)(2,1)} %bitcast.254), custom_call_target="tpu_custom_call" | custom-call | tf_op jit(solution)/shard_map/pallas_call | solution.py:107
  104.1 2.0 convert_reduce_fusion
  108.3 3.2 fusion.81
  111.5 6.3 %copy.61 = f32[16,128,640]{1,0,2:T(8,128)} copy(f32[16,128,640]{2,1,0:T(8,128)} %fusion.81) | data formatting | bytes 10485760 | tf_op jit(solution)/shard_map/cd,cij->dij/dot_general | solution.py:22
  120.4 3.7 multiply_convert_fusion
  124.1 24.1 %shard_map.121 = (bf16[128,16,128]{2,1,0:T(8,128)(2,1)}, bf16[128,16,128]{2,1,0:T(8,128)(2,1)}) custom-call(bf16[128,16,128]{2,1,0:T(8,128)(2,1)} %get-tuple-element.53.refs_0_, bf16[128,16,128]{2,1,0:T(8,128)(2,1)} %get-tuple-element.52.refs_1_), custom_call_target="tpu_custom_call" | custom-call | tf_op jit(solution)/shard_map/pallas_call | solution.py:107
  156.9 15.6 %shard_map.122 = bf16[128,16,128]{2,1,0:T(8,128)(2,1)} custom-call(bf16[128,16,128]{2,1,0:T(8,128)(2,1)} %bitcast.255), custom_call_target="tpu_custom_call" | custom-call | tf_op jit(solution)/shard_map/pallas_call | solution.py:107
  175.6 2.5 fusion.33
  178.1 2.5 add_convert_fusion.1.refs_0_
  181.1 16.3 %shard_map.125 = bf16[128,16,128]{2,1,0:T(8,128)(2,1)} custom-call(bf16[128,16,128]{2,1,0:T(8,128)(2,1)} %add_convert_fusion.1.refs_0_), custom_call_target="tpu_custom_call" | custom-call | tf_op jit(solution)/shard_map/pallas_call | solution.py:107
  198.8 2.3 convolution_convert_fusion.2
  201.1 2.3 convolution_convert_fusion.3
  207.5 24.2 %shard_map.126 = (bf16[128,16,128]{2,1,0:T(8,128)(2,1)}, bf16[128,16,128]{2,1,0:T(8,128)(2,1)}) custom-call(bf16[128,16,128]{2,1,0:T(8,128)(2,1)} %bitcast.247, bf16[128,16,128]{2,1,0:T(8,128)(2,1)} %bitcast.250), custom_call_target="tpu_custom_call" | custom-call | tf_op jit(solution)/shard_map/pallas_call | solution.py:107
  232.0 5.2 %fusion.52 = (f32[128,16,128]{2,1,0:T(8,128)S(1)}, bf16[128,16,128]{2,1,0:T(8,128)(2,1)}, f32[128,16,128]{2,1,0:T(8,128)S(1)}, f32[128,16,128]{2,1,0:T(8,128)S(1...) fusion(f32[16,128,128]{1,2,0:T(8,128)S(1)} %fusion.91, bf16[128,16,128]{2,1,0:T(8,128)(2,1)S(1)} %bitcast.236, ...), kind=kLoop, calls=%fused_computation.91 | loop fusion | flops 9961472 | bytes 14163968 | tf_op jit(solution)/shard_map/transpose(jvp())/mul | solution.py:31
  241.6 11.7 %shard_map.123 = bf16[16,128,128]{2,1,0:T(8,128)(2,1)} custom-call(bf16[16,128,128]{2,1,0:T(8,128)(2,1)} %bitcast.246), custom_call_target="tpu_custom_call" | custom-call | tf_op jit(solution)/shard_map/pallas_call | solution.py:107
  253.3 2.2 copy.68
  255.5 2.0 reshape.316
  259.4 2.7 fusion.32
  262.2 4.1 %fusion.55 = (f32[128,16,128]{2,1,0:T(8,128)}, bf16[128,16,128]{2,1,0:T(8,128)(2,1)S(1)}) fusion(f32[16,128,128]{1,2,0:T(8,128)S(1)} %copy-done.3, f32[640,16,128]{2,1,0:T(8,128)} %bitcast.229, f32[16,128]{1,0:T(8,128)S(1)} %negate_multiply_fusion.2, f32[16,128]{1,0:T(8,128)S(1)} %multiply_multiply_fusion.3, f32[16,128]{1,0:T(8,128)S(1)} %broadcast_multiply_fusion.2, ...), kind=kLoop, calls=%fused_computation.94 | loop fusion | flops 5505024 | bytes 5800448 | tf_op jit(solution)/shard_map/transpose(jvp())/mul | solution.py:31
  272.2 17.0 %shard_map.127 = bf16[128,16,128]{2,1,0:T(8,128)(2,1)} custom-call(bf16[128,16,128]{2,1,0:T(8,128)(2,1)} %add_convert_fusion.refs_0_), custom_call_target="tpu_custom_call" | custom-call | tf_op jit(solution)/shard_map/pallas_call | solution.py:107
  295.4 24.1 %shard_map.128 = (bf16[128,16,128]{2,1,0:T(8,128)(2,1)}, bf16[128,16,128]{2,1,0:T(8,128)(2,1)}) custom-call(bf16[128,16,128]{2,1,0:T(8,128)(2,1)} %bitcast.248, bf16[128,16,128]{2,1,0:T(8,128)(2,1)} %bitcast.251), custom_call_target="tpu_custom_call" | custom-call | tf_op jit(solution)/shard_map/pallas_call | solution.py:107
  319.5 3.3 convert_multiply_fusion.7
  331.1 11.6 %shard_map.129 = bf16[16,128,128]{2,1,0:T(8,128)(2,1)} custom-call(bf16[16,128,128]{2,1,0:T(8,128)(2,1)} %bitcast.260), custom_call_target="tpu_custom_call" | custom-call | tf_op jit(solution)/shard_map/pallas_call | solution.py:107
  346.2 23.3 %shard_map.130 = f32[128,16,128]{2,1,0:T(8,128)} custom-call(f32[128,16,128]{2,1,0:T(8,128)} %bitcast.242), custom_call_target="tpu_custom_call" | custom-call | tf_op jit(solution)/shard_map/pallas_call | solution.py:107
  369.5 2.0 reduce_sum.218
  371.5 25.2 %shard_map.131 = f32[128,16,128]{2,1,0:T(8,128)} custom-call(f32[1,16,128]{2,1,0:T(8,128)} %bitcast.279), custom_call_target="tpu_custom_call" | custom-call | tf_op jit(solution)/shard_map/pallas_call | solution.py:107
  (150 shorter events, 78.5 us)
Async XLA Ops:
  19.4 17.8 %copy-start.5 = (bf16[16,128,128]{2,1,0:T(8,128)(2,1)S(1)}, bf16[16,128,128]{2,1,0:T(8,128)(2,1)}, u32[]{:S(2)}) copy-start(bf16[16,128,128]{2,1,0:T(8,128)(2,1)} %shard_map.118) | copy-start | bytes 1572868
  19.4 18.2 %copy-start.22 = (bf16[2,128,640]{2,1,0:T(8,128)(2,1)S(1)}, bf16[2,128,640]{2,1,0:T(8,128)(2,1)}, u32[]{:S(2)}) copy-start(bf16[2,128,640]{2,1,0:T(8,128)(2,1)} %param.11) | copy-start | bytes 983044
  50.7 52.0 %copy-start.26 = (bf16[2,128,128]{2,1,0:T(8,128)(2,1)S(1)}, bf16[2,128,128]{2,1,0:T(8,128)(2,1)}, u32[]{:S(2)}) copy-start(bf16[2,128,128]{2,1,0:T(8,128)(2,1)} %param.13) | copy-start | bytes 196612
  78.3 1.5 copy-start.16
  79.8 0.8 copy-start.18
  101.9 0.8 copy-start.11
  103.1 1.0 copy-start.2
  107.5 0.8 copy-start.9
  111.5 6.3 %copy-start.4 = (bf16[16,128,128]{2,1,0:T(8,128)(2,1)S(1)}, bf16[16,128,128]{2,1,0:T(8,128)(2,1)}, u32[]{:S(2)}) copy-start(bf16[16,128,128]{2,1,0:T(8,128)(2,1)} %shard_map.124) | copy-start | bytes 1572868
  119.3 0.8 copy-start.13
  149.5 1.5 copy-start.20
  151.0 0.8 copy-start.21
  172.5 8.0 %copy-start.1 = (bf16[128,16,128]{2,1,0:T(8,128)(2,1)S(1)}, bf16[128,16,128]{2,1,0:T(8,128)(2,1)}, u32[]{:S(2)}) copy-start(bf16[128,16,128]{2,1,0:T(8,128)(2,1)} %shard_map.122) | copy-start | bytes 1572868
  172.5 8.2 %copy-start.14 = (bf16[128,16,128]{2,1,0:T(8,128)(2,1)S(1)}, bf16[128,16,128]{2,1,0:T(8,128)(2,1)}, u32[]{:S(2)}) copy-start(bf16[128,16,128]{2,1,0:T(8,128)(2,1)} %copy-done.13) | copy-start | bytes 1572868
  237.2 1.0 copy-start.10
  237.2 2.7 copy-start.23
  240.0 22.2 %copy-start.3 = (f32[16,128,128]{1,2,0:T(8,128)S(1)}, f32[16,128,128]{1,2,0:T(8,128)}, u32[]{:S(2)}) copy-start(f32[16,128,128]{1,2,0:T(8,128)} %copy-done.2) | copy-start | bytes 3145732
  257.5 10.4 %copy-start.12 = (bf16[128,16,128]{2,1,0:T(8,128)(2,1)S(1)}, bf16[128,16,128]{2,1,0:T(8,128)(2,1)}, u32[]{:S(2)}) copy-start(bf16[128,16,128]{2,1,0:T(8,128)(2,1)} %copy-done.11) | copy-start | bytes 1572868
  262.1 6.5 %copy-start = (bf16[128,16,128]{2,1,0:T(8,128)(2,1)S(1)}, bf16[128,16,128]{2,1,0:T(8,128)(2,1)}, u32[]{:S(2)}) copy-start(bf16[128,16,128]{2,1,0:T(8,128)(2,1)} %shard_map.120) | copy-start | bytes 1572868
  266.2 2.1 copy-start.6
  268.0 22.6 %copy-start.17 = (bf16[32,4,16,128]{3,1,2,0:T(4,128)(2,1)S(1)}, bf16[32,4,16,128]{3,1,2,0:T(4,128)(2,1)}, u32[]{:S(2)}) copy-start(bf16[32,4,16,128]{3,1,2,0:T(4,128)(2,1)} %copy-done.16) | copy-start | bytes 1572868
  268.6 22.4 %copy-start.19 = (bf16[32,4,16,128]{3,1,2,0:T(4,128)(2,1)S(1)}, bf16[32,4,16,128]{3,1,2,0:T(4,128)(2,1)}, u32[]{:S(2)}) copy-start(bf16[32,4,16,128]{3,1,2,0:T(4,128)(2,1)} %copy-done.18) | copy-start | bytes 1572868
  295.4 27.4 %copy-start.8 = (f32[128,16,128]{2,1,0:T(8,128)S(1)}, f32[128,16,128]{2,1,0:T(8,128)}, u32[]{:S(2)}) copy-start(f32[128,16,128]{2,1,0:T(8,128)} %get-tuple-element.32) | copy-start | bytes 3145732
  322.8 1.0 copy-start.15
  322.8 2.0 copy-start.24
  323.8 1.6 copy-start.25
  324.8 4.8 %copy-start.7 = (bf16[128,16,128]{2,1,0:T(8,128)(2,1)S(1)}, bf16[128,16,128]{2,1,0:T(8,128)(2,1)}, u32[]{:S(2)}) copy-start(bf16[128,16,128]{2,1,0:T(8,128)(2,1)} %copy-done.6) | copy-start | bytes 1572868

commit v3 on v1

v3 whole, which is shorter than its diff:
```python
from functools import partial

import jax
import jax.numpy as jnp
from jax import lax
from jax.experimental import pallas as pl
from jax.experimental.pallas import tpu as pltpu
from jax.sharding import PartitionSpec as P

epsilon = 1e-05
MESH = pl.DeviceIdType.MESH
f32 = jnp.float32
bf16 = jnp.bfloat16

L0, R0, X0, L1, R1, X1, DX1, DL1, DR1, DX0, DL0, DR0 = range(12)
PAIR, GRAD, POUT, GOUT, SUM1, SUM0, ALL1, ALL0 = range(12, 20)
EXCHANGES = 20


def nn(a, b):
    return lax.dot_general(a, b, (((1,), (0,)), ((), ())), preferred_element_type=f32)


def nt(a, b):
    return lax.dot_general(a, b, (((1,), (1,)), ((), ())), preferred_element_type=f32)


def tn(a, b):
    return lax.dot_general(a, b, (((0,), (0,)), ((), ())), preferred_element_type=f32)


def sigmoid(x):
    return 0.5 * jnp.tanh(0.5 * x) + 0.5


def norm(z):
    center = z - jnp.mean(z, axis=0, keepdims=True)
    scale = lax.rsqrt(jnp.mean(center * center, axis=0, keepdims=True) + epsilon)
    return center * scale, scale


def norm_back(grad, normed, scale):
    mean_grad = jnp.mean(grad, axis=0, keepdims=True)
    mean_both = jnp.mean(grad * normed, axis=0, keepdims=True)
    return scale * (grad - mean_grad - normed * mean_both)


def kernel(
    dims,
    pair,
    grad,
    chain_s,
    chain_v,
    w_in,
    w_out,
    gain_in,
    gain_mid,
    pair_out,
    grad_pair,
    sum_in,
    sum_out,
    outbox,
    inbox,
    cells_out,
    cells_in,
    sums_out,
    sums_in,
    total,
    totals,
    wt,
    wn,
    wot,
    won,
    tile_a,
    tile_b,
    tile_g,
    field,
    zhat,
    zscale,
    xhat,
    xscale,
    value_l,
    sig_l,
    value_r,
    sig_r,
    gate,
    upd,
    du,
    dgate,
    dp,
    dz,
    send,
    recv,
    own,
):
    C, rows, J, groups, across, devices = dims
    per = 2
    chunks = rows // per
    wide = per * J
    row, chan = lax.axis_index("row"), lax.axis_index("chan")
    me = row * groups + chan
    tile_i, tile_j = chan // across, lax.rem(chan, across)

    def place(to):
        return (to // groups, lax.rem(to, groups))

    barrier = pltpu.get_barrier_semaphore()

    def greet(step, carry):
        other = lax.rem(me + step, devices)
        pl.semaphore_signal(barrier, inc=1, device_id=place(other), device_id_type=MESH)
        return carry

    lax.fori_loop(1, devices, greet, 0)
    pl.semaphore_wait(barrier, devices - 1)

    def scatter(at, src, dst):
        def step(k, carry):
            other = lax.rem(me + k, devices)
            pltpu.make_async_remote_copy(
                src_ref=src.at[other],
                dst_ref=dst.at[me],
                send_sem=send.at[at],
                recv_sem=recv.at[at],
                device_id=place(other),
                device_id_type=MESH,
            ).start()
            return carry

        lax.fori_loop(1, devices, step, 0)
        pltpu.make_async_copy(src.at[me], dst.at[me], own.at[at]).start()

    def spread(at, src, dst):
        def step(k, carry):
            other = lax.rem(me + k, devices)
            pltpu.make_async_remote_copy(
                src_ref=src,
                dst_ref=dst.at[me],
                send_sem=send.at[at],
                recv_sem=recv.at[at],
                device_id=place(other),
                device_id_type=MESH,
            ).start()
            return carry

        lax.fori_loop(1, devices, step, 0)
        pltpu.make_async_copy(src, dst.at[me], own.at[at]).start()

    def landed(at, like):
        rest = like.at[pl.ds(0, devices - 1)]
        return pltpu.make_async_remote_copy(
            src_ref=rest,
            dst_ref=rest,
            send_sem=send.at[at],
            recv_sem=recv.at[at],
            device_id=(row, chan),
            device_id_type=MESH,
        )

    def arrive(at, like):
        pltpu.make_async_copy(like.at[0], like.at[0], own.at[at]).wait()
        landed(at, like).wait_recv()

    own_c = C // groups

    def tile_of(ref, other):
        first = pl.multiple_of((other // across) * rows, rows)
        left = pl.multiple_of(lax.rem(other, across) * J, J)
        return ref.at[:, pl.ds(first, rows), pl.ds(left, J)]

    def channels(ref, other):
        return ref.at[pl.ds(pl.multiple_of(other * own_c, own_c), own_c)]

    def to_cells(at, src, dst):
        def step(k, carry):
            other = lax.rem(chan + k, groups)
            pltpu.make_async_remote_copy(
                src_ref=tile_of(src, other),
                dst_ref=channels(dst, chan),
                send_sem=send.at[at],
                recv_sem=recv.at[at],
                device_id=(row, other),
                device_id_type=MESH,
            ).start()
            return carry

        lax.fori_loop(1, groups, step, 0)
        pltpu.make_async_copy(tile_of(src, chan), channels(dst, chan), own.at[at]).start()

    def from_cells(at, src, dst):
        def step(k, carry):
            other = lax.rem(chan + k, groups)
            pltpu.make_async_remote_copy(
                src_ref=channels(src, other),
                dst_ref=tile_of(dst, chan),
                send_sem=send.at[at],
                recv_sem=recv.at[at],
                device_id=(row, other),
                device_id_type=MESH,
            ).start()
            return carry

        lax.fori_loop(1, groups, step, 0)
        pltpu.make_async_copy(channels(src, chan), tile_of(dst, chan), own.at[at]).start()

    def landed_chan(at, like):
        rest = like.at[pl.ds(0, C - own_c)]
        return pltpu.make_async_remote_copy(
            src_ref=rest,
            dst_ref=rest,
            send_sem=send.at[at],
            recv_sem=recv.at[at],
            device_id=(row, chan),
            device_id_type=MESH,
        )

    def arrive_chan(at, like):
        part = like.at[pl.ds(0, own_c)]
        pltpu.make_async_copy(part, part, own.at[at]).wait()
        landed_chan(at, like).wait_recv()

    block = C // 8

    def unpack(box, tile):
        @pl.loop(0, 8)
        def _(n):
            some = box[pl.ds(n * block, block)].astype(f32)
            first = pl.multiple_of(n * block * rows, block * rows)
            tile[pl.ds(first, block * rows), :] = some.reshape(block * rows, J)

    def pack(tile, box):
        @pl.loop(0, 8)
        def _(n):
            first = pl.multiple_of(n * block * rows, block * rows)
            some = tile[pl.ds(first, block * rows), :]
            box[pl.ds(n * block, block)] = some.reshape(block, rows, J).astype(bf16)

    def load(tile, n):
        return jnp.concatenate(
            [tile[pl.ds(n * per + s, C, stride=rows), :] for s in range(per)], axis=1
        )

    def store(tile, n, value):
        for s in range(per):
            tile[pl.ds(n * per + s, C, stride=rows), :] = value[:, s * J : (s + 1) * J]

    def lanes(n):
        return pl.ds(pl.multiple_of(n * wide, wide), wide)

    columns = (chain_v[pl.ds(tile_j, 1), :] > 0).astype(f32)
    first_row = row * (rows * groups // across) + tile_i * rows

    def mask(n):
        return jnp.concatenate(
            [
                columns * (chain_s[first_row + n * per + s] > 0).astype(f32)
                for s in range(per)
            ],
            axis=1,
        )

    def matrix(box):
        high = devices // across
        tiles = box[...].reshape(high, across, rows, J)
        return jnp.concatenate(
            [tiles[:, t].reshape(high * rows, J) for t in range(across)], axis=1
        )

    def to_tiles(value, box):
        high = devices // across
        value = value.astype(bf16)
        for i in range(high):
            for t in range(across):
                box[i * across + t] = value[i * rows : (i + 1) * rows, t * J : (t + 1) * J]

    to_cells(PAIR, pair, cells_in.at[0])
    to_cells(GRAD, grad, cells_in.at[1])
    for u in range(2):
        turned = jnp.transpose(w_in[u].astype(f32)) * gain_in[pl.ds(u, 1), :]
        wt[u] = turned.astype(bf16)
        wn[u] = jnp.transpose(turned).astype(bf16)
        turned = jnp.transpose(w_out[u].astype(f32)) * gain_mid[pl.ds(u, 1), :]
        wot[u] = turned.astype(bf16)
        won[u] = jnp.transpose(turned).astype(bf16)

    def side(u, n, at, value, sig, tile):
        p = nn(wt[u, 2 * at * C : 2 * (at + 1) * C, :], zhat[u, :, lanes(n)])
        v, s = p[:C], sigmoid(p[C:])
        value[u, :, lanes(n)] = v
        sig[u, :, lanes(n)] = s
        store(tile, n, mask(n) * s * v)

    def prepare(u, at_l, at_r):
        pack(tile_a, outbox.at[at_l])
        scatter(at_l, outbox.at[at_l], inbox.at[at_l])

        @pl.loop(0, chunks)
        def _(n):
            side(u, n, 1, value_r, sig_r, tile_b)

        pack(tile_b, outbox.at[at_r])
        scatter(at_r, outbox.at[at_r], inbox.at[at_r])

        @pl.loop(0, chunks)
        def _(n):
            p = nn(wt[u, 4 * C :, :], zhat[u, :, lanes(n)])
            gate[u, :, lanes(n)] = sigmoid(p).astype(bf16).astype(f32)

    arrive_chan(PAIR, cells_in.at[0])
    unpack(cells_in.at[0], tile_b)

    @pl.loop(0, chunks)
    def _(n):
        z = load(tile_b, n)
        field[0, :, lanes(n)] = z
        normed, scale = norm(z)
        zhat[0, :, lanes(n)] = normed.astype(bf16)
        zscale[0, :, lanes(n)] = scale
        side(0, n, 0, value_l, sig_l, tile_a)

    prepare(0, L0, R0)
    arrive_chan(GRAD, cells_in.at[1])
    unpack(cells_in.at[1], tile_g)

    arrive(L0, inbox.at[L0])
    arrive(R0, inbox.at[R0])
    to_tiles(nt(matrix(inbox.at[L0]), matrix(inbox.at[R0])), outbox.at[X0])
    scatter(X0, outbox.at[X0], inbox.at[X0])

    arrive(X0, inbox.at[X0])
    unpack(inbox.at[X0], tile_b)

    @pl.loop(0, chunks)
    def _(n):
        normed, scale = norm(load(tile_b, n))
        normed = normed.astype(bf16)
        xhat[0, :, lanes(n)] = normed
        xscale[0, :, lanes(n)] = scale
        update = nn(wot[0], normed)
        upd[:, lanes(n)] = update
        z = (field[0, :, lanes(n)] + gate[0, :, lanes(n)] * update).astype(bf16).astype(f32)
        field[1, :, lanes(n)] = z
        normed, scale = norm(z)
        zhat[1, :, lanes(n)] = normed.astype(bf16)
        zscale[1, :, lanes(n)] = scale
        side(1, n, 0, value_l, sig_l, tile_a)

    prepare(1, L1, R1)
    arrive(L1, inbox.at[L1])
    arrive(R1, inbox.at[R1])
    to_tiles(tn(matrix(inbox.at[L1]), matrix(inbox.at[R1])), outbox.at[X1])
    scatter(X1, outbox.at[X1], inbox.at[X1])

    arrive(X1, inbox.at[X1])
    unpack(inbox.at[X1], tile_b)

    def finish_back(u, n, cotangent, update):
        dgate[:, lanes(n)] = (cotangent * update).astype(bf16).astype(f32)
        back = (cotangent * gate[u, :, lanes(n)]).astype(bf16)
        du[u, :, lanes(n)] = back
        dx = norm_back(nn(won[u], back), xhat[u, :, lanes(n)].astype(f32), xscale[u, :, lanes(n)])
        store(tile_a, n, dx)

    @pl.loop(0, chunks)
    def _(n):
        normed, scale = norm(load(tile_b, n))
        normed = normed.astype(bf16)
        xhat[1, :, lanes(n)] = normed
        xscale[1, :, lanes(n)] = scale
        update = nn(wot[1], normed)
        cotangent = load(tile_g, n)
        store(tile_b, n, field[1, :, lanes(n)] + gate[1, :, lanes(n)] * update)
        finish_back(1, n, cotangent, update)

    pack(tile_a, outbox.at[DX1])
    scatter(DX1, outbox.at[DX1], inbox.at[DX1])
    pack(tile_b, cells_out.at[0])
    from_cells(POUT, cells_out.at[0], pair_out)

    arrive(DX1, inbox.at[DX1])
    to_tiles(nt(matrix(inbox.at[R1]), matrix(inbox.at[DX1])), outbox.at[DL1])
    scatter(DL1, outbox.at[DL1], inbox.at[DL1])
    to_tiles(nn(matrix(inbox.at[L1]), matrix(inbox.at[DX1])), outbox.at[DR1])
    scatter(DR1, outbox.at[DR1], inbox.at[DR1])

    def side_back(u, n, at, value, sig, tile):
        s = sig[u, :, lanes(n)]
        back = load(tile, n) * mask(n) * s
        dp[2 * at * C : (2 * at + 1) * C, lanes(n)] = back.astype(bf16)
        back = back * value[u, :, lanes(n)] * (1.0 - s)
        dp[(2 * at + 1) * C : 2 * (at + 1) * C, lanes(n)] = back.astype(bf16)

    def gate_back(u):
        @pl.loop(0, chunks)
        def _(n):
            s = gate[u, :, lanes(n)]
            dp[4 * C :, lanes(n)] = (dgate[:, lanes(n)] * s * (1.0 - s)).astype(bf16)

    def left_back(u, at):
        gate_back(u)
        arrive(at, inbox.at[at])
        unpack(inbox.at[at], tile_a)

        @pl.loop(0, chunks)
        def _(n):
            side_back(u, n, 0, value_l, sig_l, tile_a)

    def prepare_back(u, n):
        grad_z = nn(wn[u], dp[:, lanes(n)])
        return norm_back(grad_z, zhat[u, :, lanes(n)].astype(f32), zscale[u, :, lanes(n)])

    left_back(1, DL1)
    arrive(DR1, inbox.at[DR1])
    unpack(inbox.at[DR1], tile_b)

    @pl.loop(0, chunks)
    def _(n):
        side_back(1, n, 1, value_r, sig_r, tile_b)
        cotangent = (load(tile_g, n) + prepare_back(1, n)).astype(bf16).astype(f32)
        dz[:, lanes(n)] = cotangent
        finish_back(0, n, cotangent, upd[:, lanes(n)])

    pack(tile_a, outbox.at[DX0])
    scatter(DX0, outbox.at[DX0], inbox.at[DX0])

    def lay(box, at, value):
        for t in range(value.shape[1] // C):
            box[pl.ds(at + t, C, stride=8), :] = value[:, t * C : (t + 1) * C]

    def send_sums(at, which, tile):
        @pl.loop(0, 8)
        def _(n):
            some = tile[pl.ds(pl.multiple_of(n * block * 8, block * 8), block * 8), :]
            sums_out[which, pl.ds(n * block, block)] = some.reshape(block, 8, C)

        scatter(at, sums_out.at[which], sums_in.at[which])

    def add_sums(at_in, at_out, which):
        arrive(at_in, sums_in.at[which])
        total[which] = jnp.sum(sums_in[which], axis=0)
        spread(at_out, total.at[which], totals.at[which])

    lay(tile_b, 0, nt(zhat[1], dp[...]))
    lay(tile_b, 5, nt(xhat[1], du[1]))
    lay(tile_b, 6, nt(xhat[0], du[0]))
    lay(tile_b, 7, jnp.zeros((C, C), f32))
    send_sums(SUM1, 0, tile_b)

    arrive(DX0, inbox.at[DX0])
    to_tiles(nn(matrix(inbox.at[DX0]), matrix(inbox.at[R0])), outbox.at[DL0])
    scatter(DL0, outbox.at[DL0], inbox.at[DL0])
    to_tiles(tn(matrix(inbox.at[DX0]), matrix(inbox.at[L0])), outbox.at[DR0])
    scatter(DR0, outbox.at[DR0], inbox.at[DR0])
    add_sums(SUM1, ALL1, 0)

    left_back(0, DL0)
    arrive(DR0, inbox.at[DR0])
    unpack(inbox.at[DR0], tile_b)

    @pl.loop(0, chunks)
    def _(n):
        side_back(0, n, 1, value_r, sig_r, tile_b)

    lay(tile_b, 0, nt(zhat[0], dp[...]))
    for t in range(5, 8):
        lay(tile_b, t, jnp.zeros((C, C), f32))
    send_sums(SUM0, 1, tile_b)

    @pl.loop(0, chunks)
    def _(n):
        store(tile_a, n, dz[:, lanes(n)] + prepare_back(0, n))

    pack(tile_a, cells_out.at[1])
    from_cells(GOUT, cells_out.at[1], grad_pair)
    add_sums(SUM0, ALL0, 1)

    def take(which, t):
        @pl.loop(0, 8)
        def _(n):
            some = totals[which, pl.ds(n * block, block)].reshape(block * 8, C)
            tile_b[pl.ds(pl.multiple_of(n * block * 8, block * 8), block * 8), :] = some

    def fetch(t):
        return tile_b[pl.ds(t, C, stride=8), :]

    arrive(ALL1, totals.at[0])
    take(0, 0)
    for t in range(5):
        sum_in[1, :, t * C : (t + 1) * C] = fetch(t)
    sum_out[1] = fetch(5)
    sum_out[0] = fetch(6)
    arrive(ALL0, totals.at[1])
    take(1, 0)
    for t in range(5):
        sum_in[0, :, t * C : (t + 1) * C] = fetch(t)

    arrive_chan(POUT, cells_out.at[0])
    arrive_chan(GOUT, cells_out.at[1])
    for at in range(12):
        landed(at, outbox.at[at]).wait_send()
    for at in range(PAIR, SUM1):
        landed_chan(at, cells_out.at[0]).wait_send()
    for at in range(SUM1, EXCHANGES):
        landed(at, sums_out.at[0]).wait_send()


def local(groups, pair, grad_out, residue_chain, gain_in, w_in, gain_mid, w_out):
    C = w_in.shape[1]
    own_c, own_rows, size = pair.shape
    devices = C
    across = 4 if groups == 16 else 2
    J = size // across
    rows = own_rows * across // groups
    cells = rows * J
    dims = (C, rows, J, groups, across, devices)
    whole = pl.BlockSpec(memory_space=pltpu.VMEM)
    far = pl.BlockSpec(memory_space=pl.ANY)
    box = (C, rows, J)
    got = pl.pallas_call(
        partial(kernel, dims),
        out_shape=[
            jax.ShapeDtypeStruct(pair.shape, bf16),
            jax.ShapeDtypeStruct(pair.shape, bf16),
            jax.ShapeDtypeStruct(w_in.shape, f32),
            jax.ShapeDtypeStruct(w_out.shape, f32),
        ],
        in_specs=[far, far, pl.BlockSpec(memory_space=pltpu.SMEM)] + [whole] * 5,
        out_specs=[far, far, whole, whole],
        scratch_shapes=[
            pltpu.VMEM((12,) + box, bf16),
            pltpu.VMEM((12,) + box, bf16),
            pltpu.VMEM((2,) + box, bf16),
            pltpu.VMEM((2,) + box, bf16),
            pltpu.VMEM((2, C, 8, C), f32),
            pltpu.VMEM((2, C, 8, C), f32),
            pltpu.VMEM((2, 8, C), f32),
            pltpu.VMEM((2, C, 8, C), f32),
            pltpu.VMEM((2, 5 * C, C), bf16),
            pltpu.VMEM((2, C, 5 * C), bf16),
            pltpu.VMEM((2, C, C), bf16),
            pltpu.VMEM((2, C, C), bf16),
            pltpu.VMEM((C * rows, J), f32),
            pltpu.VMEM((C * rows, J), f32),
            pltpu.VMEM((C * rows, J), f32),
            pltpu.VMEM((2, C, cells), f32),
            pltpu.VMEM((2, C, cells), bf16),
            pltpu.VMEM((2, 1, cells), f32),
            pltpu.VMEM((2, C, cells), bf16),
            pltpu.VMEM((2, 1, cells), f32),
            pltpu.VMEM((2, C, cells), f32),
            pltpu.VMEM((2, C, cells), f32),
            pltpu.VMEM((2, C, cells), f32),
            pltpu.VMEM((2, C, cells), f32),
            pltpu.VMEM((2, C, cells), f32),
            pltpu.VMEM((C, cells), f32),
            pltpu.VMEM((2, C, cells), bf16),
            pltpu.VMEM((C, cells), f32),
            pltpu.VMEM((5 * C, cells), bf16),
            pltpu.VMEM((C, cells), f32),
            pltpu.SemaphoreType.DMA((EXCHANGES,)),
            pltpu.SemaphoreType.DMA((EXCHANGES,)),
            pltpu.SemaphoreType.DMA((EXCHANGES,)),
        ],
        compiler_params=pltpu.CompilerParams(
            collective_id=0, has_side_effects=True, vmem_limit_bytes=60 * 2**20
        ),
    )(
        pair,
        grad_out,
        residue_chain,
        residue_chain.reshape(across, J),
        w_in,
        w_out,
        gain_in,
        gain_mid,
    )
    pair_out, grad_pair, sum_in, sum_out = got
    factor = 1.0 / size
    return (
        pair_out,
        grad_pair,
        jnp.sum(sum_in * w_in.astype(f32), axis=2) * factor,
        sum_in * gain_in[:, :, None] * factor,
        jnp.sum(sum_out * w_out.astype(f32), axis=2) * factor,
        sum_out * gain_mid[:, :, None] * factor,
    )


def solution(mesh):
    return jax.shard_map(
        partial(local, mesh.shape["chan"]),
        mesh=mesh,
        in_specs=(P("chan", "row", None), P("chan", "row", None), P(), P(), P(), P(), P()),
        out_specs=(P("chan", "row", None), P("chan", "row", None), P(), P(), P(), P()),
        check_vma=False,
    )
```

time: 539 us -> 183 us (0.34); the launches traced: 528 us -> 183 us
  waiting for transfers between devices: 297 us -> 0 us
  Pallas kernels: 0 us -> 175 us
  starting transfers between devices: 85.5 us -> 0 us
  local copies, waits for them, and re-layouts: 51.4 us -> 3.37 us
  matrix products: 32.1 us -> 0 us
  other arithmetic: 29.2 us -> 3.55 us
  blocking collectives: 17.6 us -> 0 us
  between operations: 15.3 us -> 0.67 us
    pallas_call x0 -> x1, Pallas kernels: none -> 175 us  [local(): pl.pallas_call(partial(kernel, dims), out_shape=[jax.ShapeDtypeStruct(pai...]
    all_to_all x16 -> x0, waiting for transfers between devices: 159 us -> none  [the longest x6 63.7 us: to_tiles(): return lax.all_to_all(tiles, AXES, split_axis=0, concat_axis=0, tiled=True)]
    unnamed x2 -> x0, waiting for transfers between devices: 138 us -> none
    all_to_all x16 -> x0, starting transfers between devices: 85.5 us -> none  [the longest x6 29.3 us: to_tiles(): return lax.all_to_all(tiles, AXES, split_axis=0, concat_axis=0, tiled=True)]
    dot_general x18 -> x0, matrix products: 32.1 us -> none  [the longest x6 14.5 us: finish(): update = jnp.einsum('hc,hij->cij', weight, normed)]
    all_to_all x1 -> x0, blocking collectives: 17.6 us -> none  [to_hidden(): tiles = lax.all_to_all(cells, AXES, split_axis=0, concat_axis=0, tiled=True)]
    reshape x17 -> x0, local copies, waits for them, and re-layouts: 17.3 us -> none  [the longest x10 11.4 us: to_tiles(): matrix.astype(jnp.bfloat16).reshape(size // ROWS, ROWS, size // COLS, COLS)]
    reduce_sum x11 -> x0, other arithmetic: 10.2 us -> none  [the longest x4 7.85 us: normalize(): return center * lax.rsqrt(spread + epsilon) * gain_vec[:, None, None]]
  transfers between devices with their start and end apart: 17 -> 0, of which waited for: 16 -> 0; matrix products, arithmetic and copies ran while one was open for 10% -> 0% of each run, Pallas kernels for 0% -> 0%
where the time goes in v3:
time: 183 us
  Pallas kernels  175 us (96%)
  other arithmetic  3.55 us (2%)
  local copies, waits for them, and re-layouts  3.37 us (2%)
    pallas_call x1, Pallas kernels, local(): pl.pallas_call(partial(kernel, dims), out_shape=[jax.ShapeDtypeStruct(pai...  175 us

profile of v3, /device:TPU:1, one launch (start us, length us, event | category | flops | bytes accessed | tf_op | source)
XLA Modules:
  0.0 182.7 jit_solution(16126478199771560349)
XLA Ops:
  0.6 0.0 copy-start
  0.6 175.1 %shard_map.118 = (bf16[8,64,512]{2,1,0:T(8,128)(2,1)}, bf16[8,64,512]{2,1,0:T(8,128)(2,1)}, f32[2,128,640]{2,1,0:T(8,128)}, f32[2,128,128]{2,1,0:T(8,128)}) custom-call(bf16[8,64,512]{2,1,0:T(8,128)(2,1)} %pair.1, bf16[8,64,512]{2,1,0:T(8,128)(2,1)} %grad.1, s32[512]{0:T(512)} %chain_s.1, s32[4,128]{1,0:T(4,128)} %bitcast.1, bf16[2,128,640]{2,1,0:T(8,128)(2,1)} %w_in.1, ...), custom_call_target="tpu_custom_call" | custom-call | tf_op jit(solution)/shard_map/pallas_call | solution.py:519
  175.8 0.0 copy-start.5
  175.8 0.0 copy-done
  175.8 0.7 copy-done.5
  176.4 0.0 copy-start.3
  176.4 0.0 copy-start.4
  176.4 0.0 copy-start.2
  176.4 2.2 %multiply_multiply_fusion = (f32[2,128,640]{2,1,0:T(8,128)}, f32[2,128]{1,0:T(2,128)S(1)}) fusion(f32[2,128,640]{2,1,0:T(8,128)} %get-tuple-element.12, f32[2,128]{1,0:T(2,128)S(1)} %copy-done.5, bf16[2,128,640]{2,1,0:T(8,128)(2,1)S(1)} %copy-done), kind=kLoop, calls=%fused_computation | loop fusion | flops 818944 | bytes 1640448 | tf_op jit(solution)/shard_map/mul | solution.py:583
  178.6 0.0 copy-start.6
  178.6 0.0 copy-done.3
  178.6 0.0 copy-done.4
  178.6 0.7 copy-done.6
  179.3 0.8 multiply_multiply_fusion.1
  180.1 0.6 broadcast_multiply_fusion
  180.7 0.0 copy-done.2
  180.7 0.0 copy-start.1
  180.7 0.8 copy.15
  181.5 0.4 copy-done.1
  181.9 0.8 copy.16
Async XLA Ops:
  0.6 175.1 %copy-start = (bf16[2,128,640]{2,1,0:T(8,128)(2,1)S(1)}, bf16[2,128,640]{2,1,0:T(8,128)(2,1)}, u32[]{:S(2)}) copy-start(bf16[2,128,640]{2,1,0:T(8,128)(2,1)} %w_in.1) | copy-start | bytes 983044
  175.8 0.7 copy-start.5
  176.4 2.2 %copy-start.3 = (bf16[2,128,128]{2,1,0:T(8,128)(2,1)S(1)}, bf16[2,128,128]{2,1,0:T(8,128)(2,1)}, u32[]{:S(2)}) copy-start(bf16[2,128,128]{2,1,0:T(8,128)(2,1)} %w_out.1) | copy-start | bytes 196612
  176.4 2.2 %copy-start.4 = (f32[2,128,128]{2,1,0:T(8,128)S(1)}, f32[2,128,128]{2,1,0:T(8,128)}, u32[]{:S(2)}) copy-start(f32[2,128,128]{2,1,0:T(8,128)} %get-tuple-element.13) | copy-start | bytes 393220
  176.4 4.2 %copy-start.2 = (bf16[8,64,512]{2,1,0:T(8,128)(2,1)S(1)}, bf16[8,64,512]{2,1,0:T(8,128)(2,1)}, u32[]{:S(2)}) copy-start(bf16[8,64,512]{2,1,0:T(8,128)(2,1)} %get-tuple-element.26) | copy-start | bytes 1572868
  178.6 0.7 copy-start.6
  180.7 1.2 copy-start.1

commit v4 on v3

--- a/solution.py
+++ b/solution.py
@@ -13,8 +13,12 @@
 bf16 = jnp.bfloat16
 
 L0, R0, X0, L1, R1, X1, DX1, DL1, DR1, DX0, DL0, DR0 = range(12)
-PAIR, GRAD, POUT, GOUT, SUM1, SUM0, ALL1, ALL0 = range(12, 20)
+PAIR, GRAD, POUT, GOUT = range(12, 16)
+CORES, SCATTER, GATHER, SHARE = range(16, 20)
 EXCHANGES = 20
+AT_IN = (7, 0)
+AT_OUT = (6, 5)
+SUM_ROWS = 16
 
 
 def nn(a, b):
@@ -57,16 +61,21 @@
     gain_mid,
     pair_out,
     grad_pair,
-    sum_in,
-    sum_out,
+    d_gain_in,
+    d_w_in,
+    d_gain_mid,
+    d_w_out,
     outbox,
     inbox,
     cells_out,
     cells_in,
-    sums_out,
+    sums,
+    sums_core,
+    sums_chip,
     sums_in,
     total,
     totals,
+    tile_s,
     wt,
     wn,
     wot,
@@ -86,7 +95,7 @@
     gate,
     upd,
     du,
-    dgate,
+    part,
     dp,
     dz,
     send,
@@ -94,7 +103,7 @@
     own,
 ):
     C, rows, J, groups, across, devices = dims
-    per = 2
+    per = 8
     chunks = rows // per
     wide = per * J
     row, chan = lax.axis_index("row"), lax.axis_index("chan")
@@ -130,21 +139,37 @@
         lax.fori_loop(1, devices, step, 0)
         pltpu.make_async_copy(src.at[me], dst.at[me], own.at[at]).start()
 
-    def spread(at, src, dst):
+    chips, core = devices // 2, lax.rem(me, 2)
+    chip = me // 2
+
+    def over_chips(at, source, dst):
         def step(k, carry):
-            other = lax.rem(me + k, devices)
+            other = lax.rem(chip + k, chips)
             pltpu.make_async_remote_copy(
-                src_ref=src,
-                dst_ref=dst.at[me],
+                src_ref=source(other),
+                dst_ref=dst,
                 send_sem=send.at[at],
                 recv_sem=recv.at[at],
-                device_id=place(other),
+                device_id=place(2 * other + core),
                 device_id_type=MESH,
             ).start()
             return carry
 
-        lax.fori_loop(1, devices, step, 0)
-        pltpu.make_async_copy(src, dst.at[me], own.at[at]).start()
+        lax.fori_loop(1, chips, step, 0)
+
+    def to_sibling(at, src, dst):
+        return pltpu.make_async_remote_copy(
+            src_ref=src,
+            dst_ref=dst,
+            send_sem=send.at[at],
+            recv_sem=recv.at[at],
+            device_id=place(2 * chip + 1 - core),
+            device_id_type=MESH,
+        )
+
+    def landed_chips(at):
+        rest = sums_in.at[pl.ds(0, chips - 1)]
+        return to_sibling(at, rest, rest)
 
     def landed(at, like):
         rest = like.at[pl.ds(0, devices - 1)]
@@ -162,6 +187,8 @@
         landed(at, like).wait_recv()
 
     own_c = C // groups
+    every = (0, groups)
+    quarters = [(q * groups // 4, (q + 1) * groups // 4) for q in range(4)]
 
     def tile_of(ref, other):
         first = pl.multiple_of((other // across) * rows, rows)
@@ -171,7 +198,7 @@
     def channels(ref, other):
         return ref.at[pl.ds(pl.multiple_of(other * own_c, own_c), own_c)]
 
-    def to_cells(at, src, dst):
+    def to_cells(at, src, dst, piece):
         def step(k, carry):
             other = lax.rem(chan + k, groups)
             pltpu.make_async_remote_copy(
@@ -184,10 +211,11 @@
             ).start()
             return carry
 
-        lax.fori_loop(1, groups, step, 0)
-        pltpu.make_async_copy(tile_of(src, chan), channels(dst, chan), own.at[at]).start()
-
-    def from_cells(at, src, dst):
+        lax.fori_loop(max(1, piece[0]), piece[1], step, 0)
+        if piece[0] == 0:
+            pltpu.make_async_copy(tile_of(src, chan), channels(dst, chan), own.at[at]).start()
+
+    def from_cells(at, src, dst, piece):
         def step(k, carry):
             other = lax.rem(chan + k, groups)
             pltpu.make_async_remote_copy(
@@ -200,8 +228,9 @@
             ).start()
             return carry
 
-        lax.fori_loop(1, groups, step, 0)
-        pltpu.make_async_copy(channels(src, chan), tile_of(dst, chan), own.at[at]).start()
+        lax.fori_loop(max(1, piece[0]), piece[1], step, 0)
+        if piece[0] == 0:
+            pltpu.make_async_copy(channels(src, chan), tile_of(dst, chan), own.at[at]).start()
 
     def landed_chan(at, like):
         rest = like.at[pl.ds(0, C - own_c)]
@@ -273,8 +302,8 @@
             for t in range(across):
                 box[i * across + t] = value[i * rows : (i + 1) * rows, t * J : (t + 1) * J]
 
-    to_cells(PAIR, pair, cells_in.at[0])
-    to_cells(GRAD, grad, cells_in.at[1])
+    to_cells(PAIR, pair, cells_in.at[0], every)
+    to_cells(GRAD, grad, cells_in.at[1], quarters[0])
     for u in range(2):
         turned = jnp.transpose(w_in[u].astype(f32)) * gain_in[pl.ds(u, 1), :]
         wt[u] = turned.astype(bf16)
@@ -319,13 +348,12 @@
         side(0, n, 0, value_l, sig_l, tile_a)
 
     prepare(0, L0, R0)
-    arrive_chan(GRAD, cells_in.at[1])
-    unpack(cells_in.at[1], tile_g)
-
+    to_cells(GRAD, grad, cells_in.at[1], quarters[1])
     arrive(L0, inbox.at[L0])
     arrive(R0, inbox.at[R0])
     to_tiles(nt(matrix(inbox.at[L0]), matrix(inbox.at[R0])), outbox.at[X0])
     scatter(X0, outbox.at[X0], inbox.at[X0])
+    to_cells(GRAD, grad, cells_in.at[1], quarters[2])
 
     arrive(X0, inbox.at[X0])
     unpack(inbox.at[X0], tile_b)
@@ -335,7 +363,7 @@
         normed, scale = norm(load(tile_b, n))
         normed = normed.astype(bf16)
         xhat[0, :, lanes(n)] = normed
-        xscale[0, :, lanes(n)] = scale
+        xscale[:, lanes(n)] = scale
         update = nn(wot[0], normed)
         upd[:, lanes(n)] = update
         z = (field[0, :, lanes(n)] + gate[0, :, lanes(n)] * update).astype(bf16).astype(f32)
@@ -346,42 +374,55 @@
         side(1, n, 0, value_l, sig_l, tile_a)
 
     prepare(1, L1, R1)
+    to_cells(GRAD, grad, cells_in.at[1], quarters[3])
     arrive(L1, inbox.at[L1])
     arrive(R1, inbox.at[R1])
     to_tiles(tn(matrix(inbox.at[L1]), matrix(inbox.at[R1])), outbox.at[X1])
     scatter(X1, outbox.at[X1], inbox.at[X1])
+    arrive_chan(GRAD, cells_in.at[1])
+    unpack(cells_in.at[1], tile_g)
+
+    def finish_back(u, n, cotangent):
+        back = (cotangent * gate[u, :, lanes(n)]).astype(bf16)
+        du[u, :, lanes(n)] = back
+        return nn(won[u], back)
+
+    @pl.loop(0, chunks)
+    def _(n):
+        part[:, lanes(n)] = finish_back(1, n, load(tile_g, n))
 
     arrive(X1, inbox.at[X1])
     unpack(inbox.at[X1], tile_b)
 
-    def finish_back(u, n, cotangent, update):
-        dgate[:, lanes(n)] = (cotangent * update).astype(bf16).astype(f32)
-        back = (cotangent * gate[u, :, lanes(n)]).astype(bf16)
-        du[u, :, lanes(n)] = back
-        dx = norm_back(nn(won[u], back), xhat[u, :, lanes(n)].astype(f32), xscale[u, :, lanes(n)])
-        store(tile_a, n, dx)
-
     @pl.loop(0, chunks)
     def _(n):
         normed, scale = norm(load(tile_b, n))
-        normed = normed.astype(bf16)
-        xhat[1, :, lanes(n)] = normed
-        xscale[1, :, lanes(n)] = scale
-        update = nn(wot[1], normed)
-        cotangent = load(tile_g, n)
-        store(tile_b, n, field[1, :, lanes(n)] + gate[1, :, lanes(n)] * update)
-        finish_back(1, n, cotangent, update)
+        xhat[1, :, lanes(n)] = normed.astype(bf16)
+        store(tile_a, n, norm_back(part[:, lanes(n)], normed, scale))
 
     pack(tile_a, outbox.at[DX1])
     scatter(DX1, outbox.at[DX1], inbox.at[DX1])
+
+    def gate_back(u, n, cotangent, update):
+        s = gate[u, :, lanes(n)]
+        back = (cotangent * update).astype(bf16).astype(f32)
+        dp[4 * C :, lanes(n)] = (back * s * (1.0 - s)).astype(bf16)
+
+    @pl.loop(0, chunks)
+    def _(n):
+        update = nn(wot[1], xhat[1, :, lanes(n)])
+        store(tile_b, n, field[1, :, lanes(n)] + gate[1, :, lanes(n)] * update)
+        gate_back(1, n, load(tile_g, n), update)
+
     pack(tile_b, cells_out.at[0])
-    from_cells(POUT, cells_out.at[0], pair_out)
+    from_cells(POUT, cells_out.at[0], pair_out, quarters[0])
 
     arrive(DX1, inbox.at[DX1])
     to_tiles(nt(matrix(inbox.at[R1]), matrix(inbox.at[DX1])), outbox.at[DL1])
     scatter(DL1, outbox.at[DL1], inbox.at[DL1])
     to_tiles(nn(matrix(inbox.at[L1]), matrix(inbox.at[DX1])), outbox.at[DR1])
     scatter(DR1, outbox.at[DR1], inbox.at[DR1])
+    from_cells(POUT, cells_out.at[0], pair_out, quarters[1])
 
     def side_back(u, n, at, value, sig, tile):
         s = sig[u, :, lanes(n)]
@@ -390,24 +431,22 @@
         back = back * value[u, :, lanes(n)] * (1.0 - s)
         dp[(2 * at + 1) * C : 2 * (at + 1) * C, lanes(n)] = back.astype(bf16)
 
-    def gate_back(u):
-        @pl.loop(0, chunks)
-        def _(n):
-            s = gate[u, :, lanes(n)]
-            dp[4 * C :, lanes(n)] = (dgate[:, lanes(n)] * s * (1.0 - s)).astype(bf16)
-
     def left_back(u, at):
-        gate_back(u)
         arrive(at, inbox.at[at])
         unpack(inbox.at[at], tile_a)
 
         @pl.loop(0, chunks)
         def _(n):
             side_back(u, n, 0, value_l, sig_l, tile_a)
+            part[:, lanes(n)] = nn(wn[u, :, : 2 * C], dp[: 2 * C, lanes(n)]) + nn(
+                wn[u, :, 4 * C :], dp[4 * C :, lanes(n)]
+            )
 
     def prepare_back(u, n):
-        grad_z = nn(wn[u], dp[:, lanes(n)])
-        return norm_back(grad_z, zhat[u, :, lanes(n)].astype(f32), zscale[u, :, lanes(n)])
+        right = nn(wn[u, :, 2 * C : 4 * C], dp[2 * C : 4 * C, lanes(n)])
+        return norm_back(
+            part[:, lanes(n)] + right, zhat[u, :, lanes(n)].astype(f32), zscale[u, :, lanes(n)]
+        )
 
     left_back(1, DL1)
     arrive(DR1, inbox.at[DR1])
@@ -418,42 +457,39 @@
         side_back(1, n, 1, value_r, sig_r, tile_b)
         cotangent = (load(tile_g, n) + prepare_back(1, n)).astype(bf16).astype(f32)
         dz[:, lanes(n)] = cotangent
-        finish_back(0, n, cotangent, upd[:, lanes(n)])
+        back = finish_back(0, n, cotangent)
+        store(tile_a, n, norm_back(back, xhat[0, :, lanes(n)].astype(f32), xscale[:, lanes(n)]))
 
     pack(tile_a, outbox.at[DX0])
     scatter(DX0, outbox.at[DX0], inbox.at[DX0])
 
-    def lay(box, at, value):
+    from_cells(POUT, cells_out.at[0], pair_out, quarters[2])
+
+    def lay(at, value):
         for t in range(value.shape[1] // C):
-            box[pl.ds(at + t, C, stride=8), :] = value[:, t * C : (t + 1) * C]
-
-    def send_sums(at, which, tile):
-        @pl.loop(0, 8)
-        def _(n):
-            some = tile[pl.ds(pl.multiple_of(n * block * 8, block * 8), block * 8), :]
-            sums_out[which, pl.ds(n * block, block)] = some.reshape(block, 8, C)
-
-        scatter(at, sums_out.at[which], sums_in.at[which])
-
-    def add_sums(at_in, at_out, which):
-        arrive(at_in, sums_in.at[which])
-        total[which] = jnp.sum(sums_in[which], axis=0)
-        spread(at_out, total.at[which], totals.at[which])
-
-    lay(tile_b, 0, nt(zhat[1], dp[...]))
-    lay(tile_b, 5, nt(xhat[1], du[1]))
-    lay(tile_b, 6, nt(xhat[0], du[0]))
-    lay(tile_b, 7, jnp.zeros((C, C), f32))
-    send_sums(SUM1, 0, tile_b)
+            tile_s[pl.ds(at + t, C, stride=SUM_ROWS), :] = value[:, t * C : (t + 1) * C]
+
+    lay(AT_IN[1], nt(zhat[1], dp[...]))
+    lay(AT_OUT[1], nt(xhat[1], du[1]))
+    lay(AT_OUT[0], nt(xhat[0], du[0]))
+
+    @pl.loop(0, chunks)
+    def _(n):
+        gate_back(0, n, dz[:, lanes(n)], upd[:, lanes(n)])
+
+    lay(AT_IN[0] + 4, nt(zhat[0], dp[4 * C :]))
+    for t in range(12, SUM_ROWS):
+        lay(t, jnp.zeros((C, C), f32))
 
     arrive(DX0, inbox.at[DX0])
     to_tiles(nn(matrix(inbox.at[DX0]), matrix(inbox.at[R0])), outbox.at[DL0])
     scatter(DL0, outbox.at[DL0], inbox.at[DL0])
     to_tiles(tn(matrix(inbox.at[DX0]), matrix(inbox.at[L0])), outbox.at[DR0])
     scatter(DR0, outbox.at[DR0], inbox.at[DR0])
-    add_sums(SUM1, ALL1, 0)
+    from_cells(POUT, cells_out.at[0], pair_out, quarters[3])
 
     left_back(0, DL0)
+    lay(AT_IN[0], nt(zhat[0], dp[: 2 * C]))
     arrive(DR0, inbox.at[DR0])
     unpack(inbox.at[DR0], tile_b)
 
@@ -461,47 +497,76 @@
     def _(n):
         side_back(0, n, 1, value_r, sig_r, tile_b)
 
-    lay(tile_b, 0, nt(zhat[0], dp[...]))
-    for t in range(5, 8):
-        lay(tile_b, t, jnp.zeros((C, C), f32))
-    send_sums(SUM0, 1, tile_b)
+    lay(AT_IN[0] + 2, nt(zhat[0], dp[2 * C : 4 * C]))
+    half = chips // 8
+
+    @pl.loop(0, 8)
+    def _(n):
+        first = pl.multiple_of(n * block * SUM_ROWS, block * SUM_ROWS)
+        some = tile_s[pl.ds(first, block * SUM_ROWS), :]
+        sums[pl.ds(n * half, half)] = some.reshape(half, 2, SUM_ROWS, C).astype(bf16)
+
+    to_sibling(CORES, sums.at[:, 1 - core], sums_core).start()
 
     @pl.loop(0, chunks)
     def _(n):
         store(tile_a, n, dz[:, lanes(n)] + prepare_back(0, n))
 
+    to_sibling(CORES, sums.at[:, 1 - core], sums_core).wait_recv()
+
+    @pl.loop(0, 8)
+    def _(n):
+        some = pl.ds(n * half, half)
+        sums_chip[some] = (sums[some, core].astype(f32) + sums_core[some].astype(f32)).astype(bf16)
+
+    over_chips(SCATTER, lambda other: sums_chip.at[other], sums_in.at[chip])
+    pltpu.make_async_copy(sums_chip.at[chip], sums_in.at[chip], own.at[SCATTER]).start()
     pack(tile_a, cells_out.at[1])
-    from_cells(GOUT, cells_out.at[1], grad_pair)
-    add_sums(SUM0, ALL0, 1)
-
-    def take(which, t):
-        @pl.loop(0, 8)
-        def _(n):
-            some = totals[which, pl.ds(n * block, block)].reshape(block * 8, C)
-            tile_b[pl.ds(pl.multiple_of(n * block * 8, block * 8), block * 8), :] = some
-
-    def fetch(t):
-        return tile_b[pl.ds(t, C, stride=8), :]
-
-    arrive(ALL1, totals.at[0])
-    take(0, 0)
-    for t in range(5):
-        sum_in[1, :, t * C : (t + 1) * C] = fetch(t)
-    sum_out[1] = fetch(5)
-    sum_out[0] = fetch(6)
-    arrive(ALL0, totals.at[1])
-    take(1, 0)
-    for t in range(5):
-        sum_in[0, :, t * C : (t + 1) * C] = fetch(t)
+    from_cells(GOUT, cells_out.at[1], grad_pair, every)
+
+    pltpu.make_async_copy(sums_chip.at[chip], sums_in.at[chip], own.at[SCATTER]).wait()
+    landed_chips(SCATTER).wait_recv()
+    total[...] = jnp.sum(sums_in[...].astype(f32), axis=0).astype(bf16)
+    over_chips(GATHER, lambda other: total, totals.at[core, chip])
+    pltpu.make_async_copy(total, totals.at[core, chip], own.at[GATHER]).start()
+    pltpu.make_async_copy(total, totals.at[core, chip], own.at[GATHER]).wait()
+    landed_chips(GATHER).wait_recv()
+    share = to_sibling(SHARE, totals.at[core], totals.at[core])
+    share.start()
+    share.wait_recv()
+
+    @pl.loop(0, 8)
+    def _(n):
+        some = pl.ds(n * half, half)
+        both = jnp.stack([totals[0, some], totals[1, some]], axis=1).astype(f32)
+        first = pl.multiple_of(n * block * SUM_ROWS, block * SUM_ROWS)
+        tile_s[pl.ds(first, block * SUM_ROWS), :] = both.reshape(block * SUM_ROWS, C)
+
+    factor = 1.0 / (J * across)
+    for u in range(2):
+        for at, weights, gain, d_weights, d_gain in (
+            (AT_IN[u], w_in, gain_in, d_w_in, d_gain_in),
+            (AT_OUT[u], w_out, gain_mid, d_w_out, d_gain_mid),
+        ):
+            column = jnp.transpose(jnp.broadcast_to(gain[pl.ds(u, 1), :] * factor, (C, C)))
+            both = jnp.zeros((C, C), f32)
+            for t in range(weights.shape[2] // C):
+                part = slice(t * C, (t + 1) * C)
+                rows_sum = tile_s[pl.ds(at + t, C, stride=SUM_ROWS), :]
+                d_weights[u, :, part] = rows_sum * column
+                both = both + rows_sum * weights[u, :, part].astype(f32)
+            d_gain[pl.ds(u, 1), :] = jnp.sum(jnp.transpose(both), axis=0, keepdims=True) * factor
 
     arrive_chan(POUT, cells_out.at[0])
     arrive_chan(GOUT, cells_out.at[1])
     for at in range(12):
         landed(at, outbox.at[at]).wait_send()
-    for at in range(PAIR, SUM1):
+    for at in range(PAIR, GOUT + 1):
         landed_chan(at, cells_out.at[0]).wait_send()
-    for at in range(SUM1, EXCHANGES):
-        landed(at, sums_out.at[0]).wait_send()
+    to_sibling(CORES, sums.at[:, 1 - core], sums_core).wait_send()
+    landed_chips(SCATTER).wait_send()
+    landed_chips(GATHER).wait_send()
+    share.wait_send()
 
 
 def local(groups, pair, grad_out, residue_chain, gain_in, w_in, gain_mid, w_out):
@@ -516,25 +581,30 @@
     whole = pl.BlockSpec(memory_space=pltpu.VMEM)
     far = pl.BlockSpec(memory_space=pl.ANY)
     box = (C, rows, J)
-    got = pl.pallas_call(
+    return pl.pallas_call(
         partial(kernel, dims),
         out_shape=[
             jax.ShapeDtypeStruct(pair.shape, bf16),
             jax.ShapeDtypeStruct(pair.shape, bf16),
+            jax.ShapeDtypeStruct(gain_in.shape, f32),
             jax.ShapeDtypeStruct(w_in.shape, f32),
+            jax.ShapeDtypeStruct(gain_mid.shape, f32),
             jax.ShapeDtypeStruct(w_out.shape, f32),
         ],
         in_specs=[far, far, pl.BlockSpec(memory_space=pltpu.SMEM)] + [whole] * 5,
-        out_specs=[far, far, whole, whole],
+        out_specs=[far, far] + [whole] * 4,
         scratch_shapes=[
             pltpu.VMEM((12,) + box, bf16),
             pltpu.VMEM((12,) + box, bf16),
             pltpu.VMEM((2,) + box, bf16),
             pltpu.VMEM((2,) + box, bf16),
-            pltpu.VMEM((2, C, 8, C), f32),
-            pltpu.VMEM((2, C, 8, C), f32),
-            pltpu.VMEM((2, 8, C), f32),
-            pltpu.VMEM((2, C, 8, C), f32),
+            pltpu.VMEM((C // 2, 2, SUM_ROWS, C), bf16),
+            pltpu.VMEM((C // 2, SUM_ROWS, C), bf16),
+            pltpu.VMEM((C // 2, SUM_ROWS, C), bf16),
+            pltpu.VMEM((C // 2, SUM_ROWS, C), bf16),
+            pltpu.VMEM((SUM_ROWS, C), bf16),
+            pltpu.VMEM((2, C // 2, SUM_ROWS, C), bf16),
+            pltpu.VMEM((C * SUM_ROWS, C), f32),
             pltpu.VMEM((2, 5 * C, C), bf16),
             pltpu.VMEM((2, C, 5 * C), bf16),
             pltpu.VMEM((2, C, C), bf16),
@@ -546,7 +616,7 @@
             pltpu.VMEM((2, C, cells), bf16),
             pltpu.VMEM((2, 1, cells), f32),
             pltpu.VMEM((2, C, cells), bf16),
-            pltpu.VMEM((2, 1, cells), f32),
+            pltpu.VMEM((1, cells), f32),
             pltpu.VMEM((2, C, cells), f32),
             pltpu.VMEM((2, C, cells), f32),
             pltpu.VMEM((2, C, cells), f32),
@@ -574,16 +644,6 @@
         gain_in,
         gain_mid,
     )
-    pair_out, grad_pair, sum_in, sum_out = got
-    factor = 1.0 / size
-    return (
-        pair_out,
-        grad_pair,
-        jnp.sum(sum_in * w_in.astype(f32), axis=2) * factor,
-        sum_in * gain_in[:, :, None] * factor,
-        jnp.sum(sum_out * w_out.astype(f32), axis=2) * factor,
-        sum_out * gain_mid[:, :, None] * factor,
-    )
 
 
 def solution(mesh):

time: 183 us -> 168 us (0.918)
  Pallas kernels: 175 us -> 161 us
  other arithmetic: 3.55 us -> 0 us
  local copies, waits for them, and re-layouts: 3.37 us -> 5.35 us
    pallas_call x1, Pallas kernels: 175 us -> 161 us  [local(): pl.pallas_call(partial(kernel, dims), out_shape=[jax.ShapeDtypeStruct(pai...]
    mul x3 -> x0, other arithmetic: 3.55 us -> none  [the longest x1 2.16 us: local(): sum_in * gain_in[:, :, None] * factor]
    unnamed x16, local copies, waits for them, and re-layouts: 3.37 us -> 5.35 us
where the time goes in v4:
time: 168 us; the launch traced here: 167 us
  Pallas kernels  161 us (96%)
  local copies, waits for them, and re-layouts  5.35 us (3%)
    pallas_call x1, Pallas kernels, local(): pl.pallas_call(partial(kernel, dims), out_shape=[jax.ShapeDtypeStruct(pai...  161 us
    unnamed x16, local copies, waits for them, and re-layouts  5.35 us

profile of v4, /device:TPU:1, one launch (start us, length us, event | category | flops | bytes accessed | tf_op | source)
XLA Modules:
  0.0 167.4 jit_solution(4902183730825561138)
XLA Ops:
  0.6 161.4 %shard_map.118 = (bf16[8,64,512]{2,1,0:T(8,128)(2,1)}, bf16[8,64,512]{2,1,0:T(8,128)(2,1)}, f32[2,128]{1,0:T(2,128)}, f32[2,128,640]{2,1,0:T(8,128)}, f32[2,128]{1,0:T(2,128)}, /*index=5*/f32[2,128,128]{2,1,0:T(8,128)}) custom-call(bf16[8,64,512]{2,1,0:T(8,128)(2,1)} %pair.1, bf16[8,64,512]{2,1,0:T(8,128)(2,1)} %grad.1, s32[512]{0:T(512)} %chain_s.1, ...), custom_call_target="tpu_custom_call" | custom-call | tf_op jit(solution)/shard_map/pallas_call | solution.py:584
  162.1 0.0 copy-start.1
  162.1 1.9 %copy.19 = bf16[8,64,512]{2,1,0:T(8,128)(2,1)} copy(bf16[8,64,512]{2,1,0:T(8,128)(2,1)} %get-tuple-element.12) | data formatting | bytes 1048576
  164.0 0.0 copy-done.1
  164.0 0.0 copy-start.4
  164.0 0.0 copy-start
  164.0 0.8 copy.20
  164.8 0.0 copy-done.4
  164.8 0.6 copy.21
  165.4 0.0 copy-done
  165.4 0.0 copy-start.3
  165.4 0.0 copy-start.2
  165.4 0.8 copy.22
  166.2 0.0 copy-done.3
  166.2 0.6 copy.23
  166.8 0.0 copy-done.2
  166.8 0.7 copy.24
Async XLA Ops:
  162.1 1.9 %copy-start.1 = (bf16[8,64,512]{2,1,0:T(8,128)(2,1)S(1)}, bf16[8,64,512]{2,1,0:T(8,128)(2,1)}, u32[]{:S(2)}) copy-start(bf16[8,64,512]{2,1,0:T(8,128)(2,1)} %get-tuple-element.13) | copy-start | bytes 1572868
  164.0 0.8 copy-start.4
  164.0 1.4 copy-start
  165.4 0.8 copy-start.3
  165.4 1.4 copy-start.2

commit v5 on v4

--- a/solution.py
+++ b/solution.py
@@ -15,10 +15,11 @@
 L0, R0, X0, L1, R1, X1, DX1, DL1, DR1, DX0, DL0, DR0 = range(12)
 PAIR, GRAD, POUT, GOUT = range(12, 16)
 CORES, SCATTER, GATHER, SHARE = range(16, 20)
-EXCHANGES = 20
-AT_IN = (7, 0)
-AT_OUT = (6, 5)
-SUM_ROWS = 16
+LATE_CHAN, LATE_ROW, LATE_ALL = range(20, 23)
+EXCHANGES = 23
+AT_IN1, AT_OUT, AT_GATE0 = 0, (6, 5), 7
+SUM_ROWS = 8
+LATE_ROWS = 4
 
 
 def nn(a, b):
@@ -54,17 +55,22 @@
     pair,
     grad,
     chain_s,
-    chain_v,
-    w_in,
-    w_out,
-    gain_in,
-    gain_mid,
+    chain_far,
+    w_in_far,
+    w_out_far,
+    gain_in_far,
+    gain_mid_far,
     pair_out,
     grad_pair,
     d_gain_in,
     d_w_in,
     d_gain_mid,
     d_w_out,
+    chain_v,
+    w_in,
+    w_out,
+    gain_in,
+    gain_mid,
     outbox,
     inbox,
     cells_out,
@@ -76,6 +82,14 @@
     total,
     totals,
     tile_s,
+    late,
+    late_out,
+    late_in,
+    late_part,
+    late_rows,
+    late_sum,
+    late_all,
+    columns_g,
     wt,
     wn,
     wot,
@@ -101,9 +115,10 @@
     send,
     recv,
     own,
+    fetched,
 ):
     C, rows, J, groups, across, devices = dims
-    per = 8
+    per = 16
     chunks = rows // per
     wide = per * J
     row, chan = lax.axis_index("row"), lax.axis_index("chan")
@@ -113,6 +128,20 @@
     def place(to):
         return (to // groups, lax.rem(to, groups))
 
+    small = [
+        pltpu.make_async_copy(src, dst, fetched.at[n])
+        for n, (src, dst) in enumerate(
+            (
+                (chain_far, chain_v),
+                (w_in_far, w_in),
+                (w_out_far, w_out),
+                (gain_in_far, gain_in),
+                (gain_mid_far, gain_mid),
+            )
+        )
+    ]
+    for copy in small:
+        copy.start()
     barrier = pltpu.get_barrier_semaphore()
 
     def greet(step, carry):
@@ -167,6 +196,46 @@
             device_id_type=MESH,
         )
 
+    def over_chan(at, source, dst):
+        def step(k, carry):
+            other = lax.rem(chan + k, groups)
+            pltpu.make_async_remote_copy(
+                src_ref=source(other),
+                dst_ref=dst.at[chan],
+                send_sem=send.at[at],
+                recv_sem=recv.at[at],
+                device_id=(row, other),
+                device_id_type=MESH,
+            ).start()
+            return carry
+
+        lax.fori_loop(1, groups, step, 0)
+        pltpu.make_async_copy(source(chan), dst.at[chan], own.at[at]).start()
+
+    def over_rows(at, src, dst):
+        def step(k, carry):
+            other = lax.rem(row + k, devices // groups)
+            pltpu.make_async_remote_copy(
+                src_ref=src,
+                dst_ref=dst.at[row],
+                send_sem=send.at[at],
+                recv_sem=recv.at[at],
+                device_id=(other, chan),
+                device_id_type=MESH,
+            ).start()
+            return carry
+
+        lax.fori_loop(1, devices // groups, step, 0)
+        pltpu.make_async_copy(src, dst.at[row], own.at[at]).start()
+
+    def landed_late(at, like):
+        rest = like.at[pl.ds(0, like.shape[0] - 1)]
+        return to_sibling(at, rest, rest)
+
+    def arrive_late(at, like):
+        pltpu.make_async_copy(like.at[0], like.at[0], own.at[at]).wait()
+        landed_late(at, like).wait_recv()
+
     def landed_chips(at):
         rest = sums_in.at[pl.ds(0, chips - 1)]
         return to_sibling(at, rest, rest)
@@ -276,10 +345,10 @@
     def lanes(n):
         return pl.ds(pl.multiple_of(n * wide, wide), wide)
 
-    columns = (chain_v[pl.ds(tile_j, 1), :] > 0).astype(f32)
     first_row = row * (rows * groups // across) + tile_i * rows
 
     def mask(n):
+        columns = (chain_v[pl.ds(tile_j, 1), :] > 0).astype(f32)
         return jnp.concatenate(
             [
                 columns * (chain_s[first_row + n * per + s] > 0).astype(f32)
@@ -304,6 +373,8 @@
 
     to_cells(PAIR, pair, cells_in.at[0], every)
     to_cells(GRAD, grad, cells_in.at[1], quarters[0])
+    for copy in small:
+        copy.wait()
     for u in range(2):
         turned = jnp.transpose(w_in[u].astype(f32)) * gain_in[pl.ds(u, 1), :]
         wt[u] = turned.astype(bf16)
@@ -311,6 +382,9 @@
         turned = jnp.transpose(w_out[u].astype(f32)) * gain_mid[pl.ds(u, 1), :]
         wot[u] = turned.astype(bf16)
         won[u] = jnp.transpose(turned).astype(bf16)
+        for at, gain in ((u, gain_in), (2 + u, gain_mid)):
+            scaled = gain[pl.ds(u, 1), :] * (1.0 / (J * across))
+            columns_g[at] = jnp.transpose(jnp.broadcast_to(scaled, (C, C)))
 
     def side(u, n, at, value, sig, tile):
         p = nn(wt[u, 2 * at * C : 2 * (at + 1) * C, :], zhat[u, :, lanes(n)])
@@ -469,7 +543,7 @@
         for t in range(value.shape[1] // C):
             tile_s[pl.ds(at + t, C, stride=SUM_ROWS), :] = value[:, t * C : (t + 1) * C]
 
-    lay(AT_IN[1], nt(zhat[1], dp[...]))
+    lay(AT_IN1, nt(zhat[1], dp[...]))
     lay(AT_OUT[1], nt(xhat[1], du[1]))
     lay(AT_OUT[0], nt(xhat[0], du[0]))
 
@@ -477,19 +551,45 @@
     def _(n):
         gate_back(0, n, dz[:, lanes(n)], upd[:, lanes(n)])
 
-    lay(AT_IN[0] + 4, nt(zhat[0], dp[4 * C :]))
-    for t in range(12, SUM_ROWS):
-        lay(t, jnp.zeros((C, C), f32))
+    lay(AT_GATE0, nt(zhat[0], dp[4 * C :]))
+    half = chips // 8
+
+    @pl.loop(0, 8)
+    def _(n):
+        first = pl.multiple_of(n * block * SUM_ROWS, block * SUM_ROWS)
+        some = tile_s[pl.ds(first, block * SUM_ROWS), :]
+        sums[pl.ds(n * half, half)] = some.reshape(half, 2, SUM_ROWS, C)
+
+    to_sibling(CORES, sums.at[:, 1 - core], sums_core).start()
+    to_sibling(CORES, sums.at[:, 1 - core], sums_core).wait_recv()
+
+    @pl.loop(0, 8)
+    def _(n):
+        some = pl.ds(n * half, half)
+        sums_chip[some] = sums[some, core] + sums_core[some]
+
+    over_chips(SCATTER, lambda other: sums_chip.at[other], sums_in.at[chip])
+    pltpu.make_async_copy(sums_chip.at[chip], sums_in.at[chip], own.at[SCATTER]).start()
 
     arrive(DX0, inbox.at[DX0])
     to_tiles(nn(matrix(inbox.at[DX0]), matrix(inbox.at[R0])), outbox.at[DL0])
     scatter(DL0, outbox.at[DL0], inbox.at[DL0])
     to_tiles(tn(matrix(inbox.at[DX0]), matrix(inbox.at[L0])), outbox.at[DR0])
     scatter(DR0, outbox.at[DR0], inbox.at[DR0])
+    pltpu.make_async_copy(sums_chip.at[chip], sums_in.at[chip], own.at[SCATTER]).wait()
+    landed_chips(SCATTER).wait_recv()
+    total[...] = jnp.sum(sums_in[...], axis=0)
+    over_chips(GATHER, lambda other: total, totals.at[core, chip])
+    pltpu.make_async_copy(total, totals.at[core, chip], own.at[GATHER]).start()
     from_cells(POUT, cells_out.at[0], pair_out, quarters[3])
 
     left_back(0, DL0)
-    lay(AT_IN[0], nt(zhat[0], dp[: 2 * C]))
+
+    def lay_late(at, value):
+        for t in range(value.shape[1] // C):
+            late[pl.ds(at + t, C, stride=LATE_ROWS), :] = value[:, t * C : (t + 1) * C]
+
+    lay_late(0, nt(zhat[0], dp[: 2 * C]))
     arrive(DR0, inbox.at[DR0])
     unpack(inbox.at[DR0], tile_b)
 
@@ -497,65 +597,60 @@
     def _(n):
         side_back(0, n, 1, value_r, sig_r, tile_b)
 
-    lay(AT_IN[0] + 2, nt(zhat[0], dp[2 * C : 4 * C]))
-    half = chips // 8
-
-    @pl.loop(0, 8)
-    def _(n):
-        first = pl.multiple_of(n * block * SUM_ROWS, block * SUM_ROWS)
-        some = tile_s[pl.ds(first, block * SUM_ROWS), :]
-        sums[pl.ds(n * half, half)] = some.reshape(half, 2, SUM_ROWS, C).astype(bf16)
-
-    to_sibling(CORES, sums.at[:, 1 - core], sums_core).start()
-
-    @pl.loop(0, chunks)
-    def _(n):
-        store(tile_a, n, dz[:, lanes(n)] + prepare_back(0, n))
-
-    to_sibling(CORES, sums.at[:, 1 - core], sums_core).wait_recv()
-
-    @pl.loop(0, 8)
-    def _(n):
-        some = pl.ds(n * half, half)
-        sums_chip[some] = (sums[some, core].astype(f32) + sums_core[some].astype(f32)).astype(bf16)
-
-    over_chips(SCATTER, lambda other: sums_chip.at[other], sums_in.at[chip])
-    pltpu.make_async_copy(sums_chip.at[chip], sums_in.at[chip], own.at[SCATTER]).start()
-    pack(tile_a, cells_out.at[1])
-    from_cells(GOUT, cells_out.at[1], grad_pair, every)
-
-    pltpu.make_async_copy(sums_chip.at[chip], sums_in.at[chip], own.at[SCATTER]).wait()
-    landed_chips(SCATTER).wait_recv()
-    total[...] = jnp.sum(sums_in[...].astype(f32), axis=0).astype(bf16)
-    over_chips(GATHER, lambda other: total, totals.at[core, chip])
-    pltpu.make_async_copy(total, totals.at[core, chip], own.at[GATHER]).start()
+    lay_late(2, nt(zhat[0], dp[2 * C : 4 * C]))
+    late_out[...] = late[...].reshape(late_out.shape).astype(bf16)
+    over_chan(LATE_CHAN, lambda other: late_out.at[other], late_in)
     pltpu.make_async_copy(total, totals.at[core, chip], own.at[GATHER]).wait()
     landed_chips(GATHER).wait_recv()
     share = to_sibling(SHARE, totals.at[core], totals.at[core])
     share.start()
+
+    @pl.loop(0, chunks)
+    def _(n):
+        store(tile_a, n, dz[:, lanes(n)] + prepare_back(0, n))
+
+    pack(tile_a, cells_out.at[1])
+    from_cells(GOUT, cells_out.at[1], grad_pair, (0, groups // 2))
+
+    arrive_late(LATE_CHAN, late_in)
+    late_part[...] = jnp.sum(late_in[...].astype(f32), axis=0).astype(bf16)
+    over_rows(LATE_ROW, late_part, late_rows)
+    from_cells(GOUT, cells_out.at[1], grad_pair, (groups // 2, groups))
     share.wait_recv()
 
     @pl.loop(0, 8)
     def _(n):
         some = pl.ds(n * half, half)
-        both = jnp.stack([totals[0, some], totals[1, some]], axis=1).astype(f32)
+        both = jnp.stack([totals[0, some], totals[1, some]], axis=1)
         first = pl.multiple_of(n * block * SUM_ROWS, block * SUM_ROWS)
         tile_s[pl.ds(first, block * SUM_ROWS), :] = both.reshape(block * SUM_ROWS, C)
 
-    factor = 1.0 / (J * across)
-    for u in range(2):
-        for at, weights, gain, d_weights, d_gain in (
-            (AT_IN[u], w_in, gain_in, d_w_in, d_gain_in),
-            (AT_OUT[u], w_out, gain_mid, d_w_out, d_gain_mid),
-        ):
-            column = jnp.transpose(jnp.broadcast_to(gain[pl.ds(u, 1), :] * factor, (C, C)))
-            both = jnp.zeros((C, C), f32)
-            for t in range(weights.shape[2] // C):
-                part = slice(t * C, (t + 1) * C)
-                rows_sum = tile_s[pl.ds(at + t, C, stride=SUM_ROWS), :]
-                d_weights[u, :, part] = rows_sum * column
-                both = both + rows_sum * weights[u, :, part].astype(f32)
-            d_gain[pl.ds(u, 1), :] = jnp.sum(jnp.transpose(both), axis=0, keepdims=True) * factor
+    def put(u, at, weights, d_weights, d_gain, fetch):
+        both = jnp.zeros((C, C), f32)
+        for t in range(weights.shape[2] // C):
+            columns_t = slice(t * C, (t + 1) * C)
+            rows_sum = fetch(t)
+            d_weights[u, :, columns_t] = rows_sum * columns_g[at]
+            both = both + rows_sum * weights[u, :, columns_t].astype(f32)
+        row_sum = jnp.sum(jnp.transpose(both), axis=0, keepdims=True)
+        d_gain[pl.ds(u, 1), :] = row_sum * (1.0 / (J * across))
+
+    def early(at):
+        return tile_s[pl.ds(at, C, stride=SUM_ROWS), :]
+
+    def last(t):
+        return late[pl.ds(t, C, stride=LATE_ROWS), :] if t < LATE_ROWS else early(AT_GATE0)
+
+    arrive_late(LATE_ROW, late_rows)
+    late_sum[...] = jnp.sum(late_rows[...].astype(f32), axis=0).astype(bf16)
+    over_chan(LATE_ALL, lambda other: late_sum, late_all)
+    put(1, 1, w_in, d_w_in, d_gain_in, lambda t: early(AT_IN1 + t))
+    put(0, 2, w_out, d_w_out, d_gain_mid, lambda t: early(AT_OUT[0]))
+    put(1, 3, w_out, d_w_out, d_gain_mid, lambda t: early(AT_OUT[1]))
+
+    arrive_late(LATE_ALL, late_all)
+    late[...] = late_all[...].astype(f32).reshape(late.shape)
+    put(0, 0, w_in, d_w_in, d_gain_in, last)
 
     arrive_chan(POUT, cells_out.at[0])
     arrive_chan(GOUT, cells_out.at[1])
@@ -567,6 +662,15 @@
     landed_chips(SCATTER).wait_send()
     landed_chips(GATHER).wait_send()
     share.wait_send()
+    landed_late(LATE_CHAN, late_in).wait_send()
+    landed_late(LATE_ROW, late_rows).wait_send()
+    landed_late(LATE_ALL, late_all).wait_send()
+
+
+def hand_on(*refs):
+    count = len(refs) // 2
+    for got, out in zip(refs[:count], refs[count:]):
+        out[...] = got[...]
 
 
 def local(groups, pair, grad_out, residue_chain, gain_in, w_in, gain_mid, w_out):
@@ -581,7 +685,8 @@
     whole = pl.BlockSpec(memory_space=pltpu.VMEM)
     far = pl.BlockSpec(memory_space=pl.ANY)
     box = (C, rows, J)
-    return pl.pallas_call(
+    late_rows = C // groups * LATE_ROWS
+    got = pl.pallas_call(
         partial(kernel, dims),
         out_shape=[
             jax.ShapeDtypeStruct(pair.shape, bf16),
@@ -591,20 +696,33 @@
             jax.ShapeDtypeStruct(gain_mid.shape, f32),
             jax.ShapeDtypeStruct(w_out.shape, f32),
         ],
-        in_specs=[far, far, pl.BlockSpec(memory_space=pltpu.SMEM)] + [whole] * 5,
-        out_specs=[far, far] + [whole] * 4,
+        in_specs=[far, far, pl.BlockSpec(memory_space=pltpu.SMEM)] + [far] * 5,
+        out_specs=[whole] * 6,
         scratch_shapes=[
+            pltpu.VMEM((across, J), jnp.int32),
+            pltpu.VMEM(w_in.shape, bf16),
+            pltpu.VMEM(w_out.shape, bf16),
+            pltpu.VMEM(gain_in.shape, f32),
+            pltpu.VMEM(gain_mid.shape, f32),
             pltpu.VMEM((12,) + box, bf16),
             pltpu.VMEM((12,) + box, bf16),
             pltpu.VMEM((2,) + box, bf16),
             pltpu.VMEM((2,) + box, bf16),
-            pltpu.VMEM((C // 2, 2, SUM_ROWS, C), bf16),
-            pltpu.VMEM((C // 2, SUM_ROWS, C), bf16),
-            pltpu.VMEM((C // 2, SUM_ROWS, C), bf16),
-            pltpu.VMEM((C // 2, SUM_ROWS, C), bf16),
-            pltpu.VMEM((SUM_ROWS, C), bf16),
-            pltpu.VMEM((2, C // 2, SUM_ROWS, C), bf16),
+            pltpu.VMEM((C // 2, 2, SUM_ROWS, C), f32),
+            pltpu.VMEM((C // 2, SUM_ROWS, C), f32),
+            pltpu.VMEM((C // 2, SUM_ROWS, C), f32),
+            pltpu.VMEM((C // 2, SUM_ROWS, C), f32),
+            pltpu.VMEM((SUM_ROWS, C), f32),
+            pltpu.VMEM((2, C // 2, SUM_ROWS, C), f32),
             pltpu.VMEM((C * SUM_ROWS, C), f32),
+            pltpu.VMEM((C * LATE_ROWS, C), f32),
+            pltpu.VMEM((groups, late_rows, C), bf16),
+            pltpu.VMEM((groups, late_rows, C), bf16),
+            pltpu.VMEM((late_rows, C), bf16),
+            pltpu.VMEM((devices // groups, late_rows, C), bf16),
+            pltpu.VMEM((late_rows, C), bf16),
+            pltpu.VMEM((groups, late_rows, C), bf16),
+            pltpu.VMEM((4, C, C), f32),
             pltpu.VMEM((2, 5 * C, C), bf16),
             pltpu.VMEM((2, C, 5 * C), bf16),
             pltpu.VMEM((2, C, C), bf16),
@@ -630,6 +748,7 @@
             pltpu.SemaphoreType.DMA((EXCHANGES,)),
             pltpu.SemaphoreType.DMA((EXCHANGES,)),
             pltpu.SemaphoreType.DMA((EXCHANGES,)),
+            pltpu.SemaphoreType.DMA((5,)),
         ],
         compiler_params=pltpu.CompilerParams(
             collective_id=0, has_side_effects=True, vmem_limit_bytes=60 * 2**20
@@ -644,6 +763,12 @@
         gain_in,
         gain_mid,
     )
+    return pl.pallas_call(
+        hand_on,
+        out_shape=[jax.ShapeDtypeStruct(g.shape, g.dtype) for g in got],
+        in_specs=[whole] * len(got),
+        out_specs=[whole] * len(got),
+    )(*got)
 
 
 def solution(mesh):

time: 168 us -> 161 us (0.958)
  local copies, waits for them, and re-layouts: 5.35 us -> 0 us
    unnamed x16 -> x0, local copies, waits for them, and re-layouts: 5.35 us -> none
    pallas_call x1, Pallas kernels: 161 us -> 158 us  [local(): pl.pallas_call(partial(kernel, dims), out_shape=[jax.ShapeDtypeStruct(pai...]
    pallas_call x0 -> x1, Pallas kernels: none -> 2.69 us  [local(): pl.pallas_call(hand_on, out_shape=[jax.ShapeDtypeStruct(g.shape, g.dtype)...]
where the time goes in v5:
time: 161 us
  Pallas kernels  161 us (100%)
    pallas_call x1, Pallas kernels, local(): pl.pallas_call(partial(kernel, dims), out_shape=[jax.ShapeDtypeStruct(pai...  158 us

profile of v5, /device:TPU:1, one launch (start us, length us, event | category | flops | bytes accessed | tf_op | source)
XLA Modules:
  0.0 161.2 jit_solution(10891895515003524504)
XLA Ops:
  0.6 157.9 %shard_map.118 = (bf16[8,64,512]{2,1,0:T(8,128)(2,1)}, bf16[8,64,512]{2,1,0:T(8,128)(2,1)}, f32[2,128]{1,0:T(2,128)}, f32[2,128,640]{2,1,0:T(8,128)}, f32[2,128]{1,0:T(2,128)}, /*index=5*/f32[2,128,128]{2,1,0:T(8,128)}) custom-call(bf16[8,64,512]{2,1,0:T(8,128)(2,1)} %pair.1, bf16[8,64,512]{2,1,0:T(8,128)(2,1)} %grad.1, s32[512]{0:T(512)} %chain_s.1, ...), custom_call_target="tpu_custom_call" | custom-call | tf_op jit(solution)/shard_map/pallas_call | solution.py:689
  158.5 2.7 %shard_map.119 = (bf16[8,64,512]{2,1,0:T(8,128)(2,1)}, bf16[8,64,512]{2,1,0:T(8,128)(2,1)}, f32[2,128]{1,0:T(2,128)}, f32[2,128,640]{2,1,0:T(8,128)}, f32[2,128]{1,0:T(2,128)}, /*index=5*/f32[2,128,128]{2,1,0:T(8,128)}) custom-call(bf16[8,64,512]{2,1,0:T(8,128)(2,1)} %get-tuple-element.12.refs_0_, bf16[8,64,512]{2,1,0:T(8,128)(2,1)} %get-tuple-element.13.refs_1_, ...), custom_call_target="tpu_custom_call" | custom-call | tf_op jit(solution)/shard_map/pallas_call | solution.py:766

commit v6 on v5

--- a/solution.py
+++ b/solution.py
@@ -198,7 +198,7 @@
 
     def over_chan(at, source, dst):
         def step(k, carry):
-            other = lax.rem(chan + k, groups)
+            other = lax.rem(chan + 5 * k, groups)
             pltpu.make_async_remote_copy(
                 src_ref=source(other),
                 dst_ref=dst.at[chan],
@@ -269,7 +269,7 @@
 
     def to_cells(at, src, dst, piece):
         def step(k, carry):
-            other = lax.rem(chan + k, groups)
+            other = lax.rem(chan + 5 * k, groups)
             pltpu.make_async_remote_copy(
                 src_ref=tile_of(src, other),
                 dst_ref=channels(dst, chan),
@@ -286,7 +286,7 @@
 
     def from_cells(at, src, dst, piece):
         def step(k, carry):
-            other = lax.rem(chan + k, groups)
+            other = lax.rem(chan + 5 * k, groups)
             pltpu.make_async_remote_copy(
                 src_ref=channels(src, other),
                 dst_ref=tile_of(dst, chan),

time: 161 us -> 158 us (0.981)
  Pallas kernels: 161 us -> 158 us
    pallas_call x1, Pallas kernels: 158 us -> 155 us  [local(): pl.pallas_call(partial(kernel, dims), out_shape=[jax.ShapeDtypeStruct(pai...]
where the time goes in v6:
time: 158 us
  Pallas kernels  158 us (100%)
    pallas_call x1, Pallas kernels, local(): pl.pallas_call(partial(kernel, dims), out_shape=[jax.ShapeDtypeStruct(pai...  155 us

profile of v6, /device:TPU:1, one launch (start us, length us, event | category | flops | bytes accessed | tf_op | source)
XLA Modules:
  0.0 158.3 jit_solution(3446704246799573823)
XLA Ops:
  0.6 154.9 %shard_map.118 = (bf16[8,64,512]{2,1,0:T(8,128)(2,1)}, bf16[8,64,512]{2,1,0:T(8,128)(2,1)}, f32[2,128]{1,0:T(2,128)}, f32[2,128,640]{2,1,0:T(8,128)}, f32[2,128]{1,0:T(2,128)}, /*index=5*/f32[2,128,128]{2,1,0:T(8,128)}) custom-call(bf16[8,64,512]{2,1,0:T(8,128)(2,1)} %pair.1, bf16[8,64,512]{2,1,0:T(8,128)(2,1)} %grad.1, s32[512]{0:T(512)} %chain_s.1, ...), custom_call_target="tpu_custom_call" | custom-call | tf_op jit(solution)/shard_map/pallas_call | solution.py:689
  155.6 2.7 %shard_map.119 = (bf16[8,64,512]{2,1,0:T(8,128)(2,1)}, bf16[8,64,512]{2,1,0:T(8,128)(2,1)}, f32[2,128]{1,0:T(2,128)}, f32[2,128,640]{2,1,0:T(8,128)}, f32[2,128]{1,0:T(2,128)}, /*index=5*/f32[2,128,128]{2,1,0:T(8,128)}) custom-call(bf16[8,64,512]{2,1,0:T(8,128)(2,1)} %get-tuple-element.12.refs_0_, bf16[8,64,512]{2,1,0:T(8,128)(2,1)} %get-tuple-element.13.refs_1_, ...), custom_call_target="tpu_custom_call" | custom-call | tf_op jit(solution)/shard_map/pallas_call | solution.py:766

commit v7 on v6

--- a/solution.py
+++ b/solution.py
@@ -320,14 +320,14 @@
     block = C // 8
 
     def unpack(box, tile):
-        @pl.loop(0, 8)
+        @pl.loop(0, 8, unroll=4)
         def _(n):
             some = box[pl.ds(n * block, block)].astype(f32)
             first = pl.multiple_of(n * block * rows, block * rows)
             tile[pl.ds(first, block * rows), :] = some.reshape(block * rows, J)
 
     def pack(tile, box):
-        @pl.loop(0, 8)
+        @pl.loop(0, 8, unroll=4)
         def _(n):
             first = pl.multiple_of(n * block * rows, block * rows)
             some = tile[pl.ds(first, block * rows), :]
@@ -554,7 +554,7 @@
     lay(AT_GATE0, nt(zhat[0], dp[4 * C :]))
     half = chips // 8
 
-    @pl.loop(0, 8)
+    @pl.loop(0, 8, unroll=4)
     def _(n):
         first = pl.multiple_of(n * block * SUM_ROWS, block * SUM_ROWS)
         some = tile_s[pl.ds(first, block * SUM_ROWS), :]
@@ -563,7 +563,7 @@
     to_sibling(CORES, sums.at[:, 1 - core], sums_core).start()
     to_sibling(CORES, sums.at[:, 1 - core], sums_core).wait_recv()
 
-    @pl.loop(0, 8)
+    @pl.loop(0, 8, unroll=4)
     def _(n):
         some = pl.ds(n * half, half)
         sums_chip[some] = sums[some, core] + sums_core[some]
@@ -618,7 +618,7 @@
     from_cells(GOUT, cells_out.at[1], grad_pair, (groups // 2, groups))
     share.wait_recv()
 
-    @pl.loop(0, 8)
+    @pl.loop(0, 8, unroll=4)
     def _(n):
         some = pl.ds(n * half, half)
         both = jnp.stack([totals[0, some], totals[1, some]], axis=1)

time: 158 us -> 159 us (level)
  no operation moved by 1% of the time
where the time goes in v7:
time: 159 us; the launch traced here: 158 us
  Pallas kernels  158 us (99%)
    pallas_call x1, Pallas kernels, local(): pl.pallas_call(partial(kernel, dims), out_shape=[jax.ShapeDtypeStruct(pai...  155 us

profile of v7, /device:TPU:1, one launch (start us, length us, event | category | flops | bytes accessed | tf_op | source)
XLA Modules:
  0.0 158.4 jit_solution(4197036555540350046)
XLA Ops:
  0.6 155.1 %shard_map.118 = (bf16[8,64,512]{2,1,0:T(8,128)(2,1)}, bf16[8,64,512]{2,1,0:T(8,128)(2,1)}, f32[2,128]{1,0:T(2,128)}, f32[2,128,640]{2,1,0:T(8,128)}, f32[2,128]{1,0:T(2,128)}, /*index=5*/f32[2,128,128]{2,1,0:T(8,128)}) custom-call(bf16[8,64,512]{2,1,0:T(8,128)(2,1)} %pair.1, bf16[8,64,512]{2,1,0:T(8,128)(2,1)} %grad.1, s32[512]{0:T(512)} %chain_s.1, ...), custom_call_target="tpu_custom_call" | custom-call | tf_op jit(solution)/shard_map/pallas_call | solution.py:689
  155.7 2.7 %shard_map.119 = (bf16[8,64,512]{2,1,0:T(8,128)(2,1)}, bf16[8,64,512]{2,1,0:T(8,128)(2,1)}, f32[2,128]{1,0:T(2,128)}, f32[2,128,640]{2,1,0:T(8,128)}, f32[2,128]{1,0:T(2,128)}, /*index=5*/f32[2,128,128]{2,1,0:T(8,128)}) custom-call(bf16[8,64,512]{2,1,0:T(8,128)(2,1)} %get-tuple-element.12.refs_0_, bf16[8,64,512]{2,1,0:T(8,128)(2,1)} %get-tuple-element.13.refs_1_, ...), custom_call_target="tpu_custom_call" | custom-call | tf_op jit(solution)/shard_map/pallas_call | solution.py:766
